TPU v7x, 512 devices: a whole 4x8x8 slice. The times are simulated.
512 devices in a mesh: wide: 32 (over x, y), narrow: 16 (over z, core).
Axes of the slice: x: 4, y: 8, z: 8, core: 2. Of those that a mesh axis runs over, the one named last changes fastest.
Arguments:
- hidden: bfloat16 [512, 4096], P('wide', 'narrow'), may hold values from -90 to 90
- head_weights: bfloat16 [4096, 303104], P(None, ('wide', 'narrow')), may hold values from -0.09375 to 0.09375
- token_ids: int32 [256], replicated, may hold values from 0 to 151551
- kl_weight: float32 [256], replicated, may hold values from 4 to 32
- advantage: float32 [256], replicated, may hold values from -12 to 12
Outputs:
- hidden_grad: float32 [4096, 512], P('narrow', 'wide')
- mixture_lse: float32 [256], replicated
- divergence: float32 [256], replicated
All inputs are finite; a program needn't handle non-finite values.
Results may differ from a plain program's by a relative error of at most 0.012.
Values may be sent and summed in bfloat16 or wider, within the bound.
No kernel may reach another device: no remote copies, remote signals or barrier semaphores. Data moves between devices by JAX's collectives and lax.ppermute only.
A program may use at most 64 MiB of HBM per device.

v0:
```python
import jax
import jax.numpy as jnp
from jax import lax
from jax.sharding import Mesh
from jax.sharding import PartitionSpec as P

WIDE = ("wide_0", "wide_1")
NARROW = ("narrow_0", "narrow_1")
WIDE_NARROW = ("wide_0", "wide_1", "narrow_0", "narrow_1")


BETA = 0.2


def partner(block, axis, bit):
    count = lax.axis_size(axis)
    route = []
    for low in range(count):
        high = low | 1 << bit
        if high != low and high < count:
            route += [(low, high), (high, low)]
    return lax.ppermute(block, axis, route)


def laid_out(parts, dim):
    parts = jnp.moveaxis(parts, 0, dim)
    lengths = parts.shape
    return parts.reshape(*lengths[:dim], lengths[dim] * lengths[dim + 1], *lengths[dim + 2 :])


def copy_for_each(shard, axis):
    size = lax.axis_size(axis)
    return lax.all_to_all(
        jnp.broadcast_to(shard[None], (size, *shard.shape)), axis, 0, 0, tiled=True
    )


def gathered_copies(shard, axis, dim):
    return laid_out(copy_for_each(shard, axis), dim)


def all_in_one(shard, axis):
    leaves = jax.tree.leaves(shard)
    sequence = sorted(range(len(leaves)), key=lambda k: -leaves[k].size)
    width = (1, *leaves[sequence[0]].shape)[-1]
    lines = [
        jnp.pad(leaves[k].reshape(-1), (0, -leaves[k].size % width)).reshape(-1, width)
        for k in sequence
    ]
    both, at, found = (lax.all_gather(jnp.concatenate(lines), axis), 0, {})
    for k, line in zip(sequence, lines):
        slab = both[:, at : at + len(line)].reshape(len(both), -1)
        found[k] = slab[:, : leaves[k].size].reshape(-1, *leaves[k].shape)
        at += len(line)
    numbers = iter(range(len(leaves)))
    return jax.tree.map(lambda _: found[next(numbers)], shard)


def merged_by_axis(shard, axes, combine):
    for axis in axes:
        pieces = all_in_one(shard, axis)
        shard = jax.tree.map(lambda part: part[0], pieces)
        for k in range(1, lax.axis_size(axis)):
            shard = combine(shard, jax.tree.map(lambda part: part[k], pieces))
    return shard


def in_blocks(shard, dim, size):
    before, after = (shard.shape[:dim], shard.shape[dim + 1 :])
    return jnp.moveaxis(shard.reshape(*before, size, -1, *after), dim, 0)


def summed_on_arrival(shard, axis, dim):
    size = lax.axis_size(axis)
    parts = lax.all_to_all(in_blocks(shard, dim, size), axis, 0, 0, tiled=True)
    return jnp.sum(parts.astype(jnp.float32), axis=0)


def combine_stats(earlier, later):
    policy_top = jnp.maximum(earlier[0], later[0])
    mixture_top = jnp.maximum(earlier[3], later[3])
    left_policy = jnp.exp(earlier[0] - policy_top)
    right_policy = jnp.exp(later[0] - policy_top)
    left_mixture = jnp.exp(earlier[3] - mixture_top)
    right_mixture = jnp.exp(later[3] - mixture_top)
    return (
        policy_top,
        earlier[1] * left_policy + later[1] * right_policy,
        earlier[2] * left_policy + later[2] * right_policy,
        mixture_top,
        earlier[4] * left_mixture + later[4] * right_mixture,
    )


def body(hidden, head_weights, token_ids, kl_weight, advantage):
    wide_count = lax.axis_size(WIDE)
    narrow_count = lax.axis_size(NARROW)
    half_count = wide_count // 2
    half_bits = half_count.bit_length() - 1
    wide_index = lax.axis_index(WIDE)
    narrow_index = lax.axis_index(NARROW)
    is_reference = wide_index >= half_count
    block_width = head_weights.shape[1]
    col_start = (wide_index % half_count * narrow_count + narrow_index) * block_width
    gathered = hidden
    for bit_number in range(half_bits):
        partner_rows = partner(gathered, WIDE, bit_number)
        upper_bit = wide_index // (1 << bit_number) % 2 == 1
        gathered = jnp.where(
            upper_bit,
            jnp.concatenate([partner_rows, gathered], 0),
            jnp.concatenate([gathered, partner_rows], 0),
        )
    row_total = gathered.shape[0]
    own_logits = jnp.dot(
        gathered_copies(gathered, NARROW, 1), head_weights, preferred_element_type=jnp.float32
    )
    partner_logits = partner(own_logits, WIDE, half_bits)
    policy_logits = jnp.where(is_reference, partner_logits, own_logits)
    ref_logits = jnp.where(is_reference, own_logits, partner_logits)
    mixed_logits = (1.0 - BETA) * policy_logits + BETA * ref_logits
    rows_owned = ((jnp.arange(row_total) >= row_total // 2) == is_reference).astype(jnp.float32)
    local_policy = jnp.max(policy_logits, 1)
    local_mixture = jnp.max(mixed_logits, 1)
    policy_exp = jnp.exp(policy_logits - local_policy[:, None])
    mixture_exp = jnp.exp(mixed_logits - local_mixture[:, None])
    policy_top, policy_sum, cross_sum, mixture_top, mixture_sum = merged_by_axis(
        (
            local_policy,
            rows_owned * jnp.sum(policy_exp, 1),
            rows_owned * jnp.sum(policy_exp * (policy_logits - mixed_logits), 1),
            local_mixture,
            rows_owned * jnp.sum(mixture_exp, 1),
        ),
        WIDE_NARROW,
        combine_stats,
    )
    policy_lse = policy_top + jnp.log(policy_sum)
    mixture_lse = mixture_top + jnp.log(mixture_sum)
    divergence = cross_sum / policy_sum - policy_lse + mixture_lse
    policy_prob = jnp.exp(policy_logits - policy_lse[:, None])
    mixture_prob = jnp.exp(mixed_logits - mixture_lse[:, None])
    log_gap = policy_logits - policy_lse[:, None] - mixed_logits + mixture_lse[:, None]
    chosen = (
        token_ids[:, None] == col_start + jnp.arange(block_width, dtype=jnp.int32)[None, :]
    ).astype(jnp.float32)
    prob_shift = mixture_prob - policy_prob
    policy_grad = kl_weight[:, None] * (
        policy_prob * (log_gap - divergence[:, None]) + (1.0 - BETA) * prob_shift
    ) - advantage[:, None] * (chosen - policy_prob)
    ref_grad = BETA * kl_weight[:, None] * prob_shift
    own_grad = jnp.where(is_reference, ref_grad, policy_grad).astype(jnp.bfloat16)
    contract = (((1,), (1,)), ((), ()))
    summed = lax.dot_general(head_weights, own_grad, contract, preferred_element_type=jnp.float32)
    for bit_number in reversed(range(half_bits)):
        half_size = summed.shape[1] // 2
        upper_bit = wide_index // (1 << bit_number) % 2 == 1
        kept_half = jnp.where(upper_bit, summed[:, half_size:], summed[:, :half_size])
        sent_half = jnp.where(upper_bit, summed[:, :half_size], summed[:, half_size:])
        summed = kept_half + partner(sent_half.astype(jnp.bfloat16), WIDE, bit_number).astype(
            sent_half.dtype
        )
    hidden_grad = summed_on_arrival(summed.astype(jnp.bfloat16), NARROW, 0)
    return (hidden_grad, mixture_lse, divergence)


def solution(mesh):
    finer = Mesh(mesh.devices.reshape(4, 8, 8, 2), ("wide_0", "wide_1", "narrow_0", "narrow_1"))
    return jax.shard_map(
        body,
        mesh=finer,
        in_specs=(P(WIDE, NARROW), P(None, WIDE_NARROW), P(), P(), P()),
        out_specs=(P(NARROW, WIDE), P(), P()),
        check_vma=False,
    )
```

profile of v0, /device:TPU:1, one launch (start us, length us, event | category | flops | bytes accessed | tf_op | source)
XLA Modules:
  0.0 277.8 jit_solution(11887816465627759585)
XLA Ops:
  0.6 4.0 %collective-permute-start = (bf16[16,256]{1,0:T(8,128)(2,1)}, bf16[16,256]{1,0:T(8,128)(2,1)S(1)}, u32[]{:S(2)}, u32[]{:S(2)}) collective-permute-start(bf16[16,256]{1,0:T(8,128)(2,1)} %param.5), channel_id=1, source_target_pairs={{0,16},{16,0},{32,48},{48,32},{64,80},{80,64},{96,112},{112,96},{1... | collective-permute-start | bytes 24584 | tf_op jit(solution)/shard_map/ppermute | solution.py:22
  4.7 1.2 collective-permute-done
  5.9 0.8 maximum_select_fusion.3
  6.7 4.4 %collective-permute-start.1 = (bf16[32,256]{1,0:T(8,128)(2,1)S(1)}, bf16[32,256]{1,0:T(8,128)(2,1)S(1)}, u32[]{:S(2)}, u32[]{:S(2)}) collective-permute-start(bf16[32,256]{1,0:T(8,128)(2,1)S(1)} %maximum_select_fusion.3), channel_id=1, source_target_pairs={{0,32},{32,0},{16,48},{48,16},{64,96},{96,64},{80,112},{112,80},{1... | collective-permute-start | bytes 49160 | tf_op jit(solution)/shard_map/ppermute | solution.py:22
  11.1 1.1 collective-permute-done.1
  12.2 7.5 %collective-permute-start.2 = (bf16[64,256]{1,0:T(8,128)(2,1)S(1)}, bf16[64,256]{1,0:T(8,128)(2,1)S(1)}, u32[]{:S(2)}, u32[]{:S(2)}) collective-permute-start(bf16[64,256]{1,0:T(8,128)(2,1)S(1)} %maximum_select_fusion.2), channel_id=1, source_target_pairs={{0,64},{64,0},{16,80},{80,16},{32,96},{96,32},{48,112},{112,48},{1... | collective-permute-start | bytes 98312 | tf_op jit(solution)/shard_map/ppermute | solution.py:22
  19.7 1.3 collective-permute-done.2
  21.0 3.1 %collective-permute-start.3 = (bf16[128,256]{1,0:T(8,128)(2,1)S(1)}, bf16[128,256]{1,0:T(8,128)(2,1)S(1)}, u32[]{:S(2)}, u32[]{:S(2)}) collective-permute-start(bf16[128,256]{1,0:T(8,128)(2,1)S(1)} %maximum_select_fusion.1), channel_id=1, source_target_pairs={{0,128},{128,0},{16,144},{144,16},{32,160},{160,32},{48,176},{176,... | collective-permute-start | bytes 196616 | tf_op jit(solution)/shard_map/ppermute | solution.py:22
  24.2 1.9 collective-permute-done.3
  26.1 0.1 copy.9
  26.2 0.0 copy-start
  26.2 0.2 broadcast_in_dim.2
  26.4 66.5 %all_to_all.10 = bf16[16,256,256]{1,2,0:T(8,128)(2,1)S(1)} all-to-all(bf16[16,256,256]{1,2,0:T(8,128)(2,1)S(1)} %broadcast_in_dim.2), channel_id=1, replica_groups=mesh['wide_0'=4,'wide_1'=8,'narrow_0'=8,'narrow_1'=2] {'narrow_0','narro..., dimensions={0} | all-to-all | bytes 4194304 | tf_op jit(solution)/shard_map/all_to_all | solution.py:33
  92.9 0.0 copy-done
  92.9 1.4 fusion.213
  94.3 4.7 %collective-permute-start.4 = (f32[256,592]{0,1:T(8,128)S(1)}, f32[256,592]{0,1:T(8,128)S(1)}, u32[]{:S(2)}, u32[]{:S(2)}) collective-permute-start(f32[256,592]{0,1:T(8,128)S(1)} %fusion.213), channel_id=1, source_target_pairs={{0,256},{256,0},{16,272},{272,16},{32,288},{288,32},{48,304},{304,... | collective-permute-start | bytes 1818632 | tf_op jit(solution)/shard_map/ppermute | solution.py:22
  99.0 0.0 copy-done.1
  99.0 0.0 copy-start.4
  99.0 0.0 copy-start.5
  99.0 13.3 %collective-permute-done.4 = f32[256,592]{0,1:T(8,128)S(1)} collective-permute-done((f32[256,592]{0,1:T(8,128)S(1)}, f32[256,592]{0,1:T(8,128)S(1)}, u32[]{:S(2)}, u32[]{:S(2)}) %collective-permute-start.4) | collective-permute-done | bytes 606240 | tf_op jit(solution)/shard_map/ppermute | solution.py:22
  112.4 0.2 fusion.211
  112.5 0.1 reduce_max.18
  112.6 0.2 multiply_reduce_fusion
  112.9 9.4 %all-gather.4 = f32[4,5,256]{2,1,0:T(8,128)S(1)} all-gather(f32[1,5,256]{2,1,0:T(8,128)S(1)} %bitcast.1068), channel_id=2, replica_groups=mesh['wide_0'=4,'wide_1'=8,'narrow_0'=8,'narrow_1'=2] {'wide_0'}, dimensions={0}, use_global_device_ids=true | all-gather | bytes 25600 | tf_op jit(solution)/shard_map/all_gather | solution.py:50
  122.4 19.8 %all-gather.5 = f32[8,5,256]{2,1,0:T(8,128)S(1)} all-gather(f32[1,5,256]{2,1,0:T(8,128)S(1)} %bitcast.1069), channel_id=3, replica_groups=mesh['wide_0'=4,'wide_1'=8,'narrow_0'=8,'narrow_1'=2] {'wide_1'}, dimensions={0}, use_global_device_ids=true | all-gather | bytes 46080 | tf_op jit(solution)/shard_map/all_gather | solution.py:50
  142.3 18.2 %all-gather.6 = f32[8,5,256]{2,1,0:T(8,128)S(1)} all-gather(f32[1,5,256]{2,1,0:T(8,128)S(1)} %bitcast.1070), channel_id=4, replica_groups=mesh['wide_0'=4,'wide_1'=8,'narrow_0'=8,'narrow_1'=2] {'narrow_0'}, dimensions={0}, use_global_device_ids=true | all-gather | bytes 46080 | tf_op jit(solution)/shard_map/all_gather | solution.py:50
  160.7 17.0 %all-gather.7 = f32[2,5,256]{2,1,0:T(8,128)S(1)} all-gather(f32[1,5,256]{2,1,0:T(8,128)S(1)} %bitcast.1071), channel_id=5, replica_groups=mesh['wide_0'=4,'wide_1'=8,'narrow_0'=8,'narrow_1'=2] {'narrow_1'}, dimensions={0}, use_global_device_ids=true | all-gather | bytes 15360 | tf_op jit(solution)/shard_map/all_gather | solution.py:50
  177.7 0.0 copy-start.2
  177.7 0.0 copy-start.3
  177.8 4.6 %convolution_bitcast_fusion = f32[4096,256]{0,1:T(8,128)S(1)} fusion(bf16[4096,592]{0,1:T(8,128)(2,1)} %param.6, f32[256,592]{0,1:T(8,128)S(1)} %get-tuple-element.25, f32[256,592]{0,1:T(8,128)S(1)} %get-tuple-element.26, s32[256]{0:T(256)S(1)} %copy-done.4, f32[256]{0:T(256)S(1)} %copy-done.5, f32[256]{0:T(256)S(1)} %get-tuple-element.6, ...), kind=kOutput, calls=%fused_computation | convolution fusion | flops 1244241920 | bytes 10265921 | tf_op jit(solution)/shard_map/dot_general | solution.py:154
  182.4 0.0 copy-done.2
  182.4 0.0 copy-done.3
  182.4 0.2 select_convert_fusion
  182.6 2.8 %collective-permute-start.5 = (bf16[4096,128]{0,1:T(8,128)(2,1)S(1)}, bf16[4096,128]{0,1:T(8,128)(2,1)S(1)}, u32[]{:S(2)}, u32[]{:S(2)}) collective-permute-start(bf16[4096,128]{0,1:T(8,128)(2,1)S(1)} %select_convert_fusion), channel_id=1, source_target_pairs={{0,128},{128,0},{16,144},{144,16},{32,160},{160,32},{48,176},{176,... | collective-permute-start | bytes 3145736 | tf_op jit(solution)/shard_map/ppermute | solution.py:22
  185.4 23.5 %collective-permute-done.5 = bf16[4096,128]{0,1:T(8,128)(2,1)S(1)} collective-permute-done((bf16[4096,128]{0,1:T(8,128)(2,1)S(1)}, bf16[4096,128]{0,1:T(8,128)(2,1)S(1)}, u32[]{:S(2)}, u32[]{:S(2)}) %collective-permute-start.5) | collective-permute-done | bytes 1048608 | tf_op jit(solution)/shard_map/ppermute | solution.py:22
  208.9 0.3 convert_add_fusion
  209.2 0.1 select_convert_fusion.1
  209.3 6.1 %collective-permute-start.6 = (bf16[4096,64]{0,1:T(8,128)(2,1)S(1)}, bf16[4096,64]{0,1:T(8,128)(2,1)S(1)}, u32[]{:S(2)}, u32[]{:S(2)}) collective-permute-start(bf16[4096,64]{0,1:T(8,128)(2,1)S(1)} %select_convert_fusion.1), channel_id=1, source_target_pairs={{0,64},{64,0},{16,80},{80,16},{32,96},{96,32},{48,112},{112,48},{1... | collective-permute-start | bytes 1572872 | tf_op jit(solution)/shard_map/ppermute | solution.py:22
  215.5 19.1 %collective-permute-done.6 = bf16[4096,64]{0,1:T(8,128)(2,1)S(1)} collective-permute-done((bf16[4096,64]{0,1:T(8,128)(2,1)S(1)}, bf16[4096,64]{0,1:T(8,128)(2,1)S(1)}, u32[]{:S(2)}, u32[]{:S(2)}) %collective-permute-start.6) | collective-permute-done | bytes 524320 | tf_op jit(solution)/shard_map/ppermute | solution.py:22
  234.6 0.2 convert_add_fusion.1
  234.7 0.1 select_convert_fusion.3
  234.8 9.7 %collective-permute-start.7 = (bf16[4096,32]{0,1:T(8,128)(2,1)S(1)}, bf16[4096,32]{0,1:T(8,128)(2,1)S(1)}, u32[]{:S(2)}, u32[]{:S(2)}) collective-permute-start(bf16[4096,32]{0,1:T(8,128)(2,1)S(1)} %select_convert_fusion.3), channel_id=1, source_target_pairs={{0,32},{32,0},{16,48},{48,16},{64,96},{96,64},{80,112},{112,80},{1... | collective-permute-start | bytes 786440 | tf_op jit(solution)/shard_map/ppermute | solution.py:22
  244.5 11.7 %collective-permute-done.7 = bf16[4096,32]{0,1:T(8,128)(2,1)S(1)} collective-permute-done((bf16[4096,32]{0,1:T(8,128)(2,1)S(1)}, bf16[4096,32]{0,1:T(8,128)(2,1)S(1)}, u32[]{:S(2)}, u32[]{:S(2)}) %collective-permute-start.7) | collective-permute-done | bytes 262176 | tf_op jit(solution)/shard_map/ppermute | solution.py:22
  256.3 0.1 convert_add_fusion.2
  256.4 1.9 collective-permute-start.8
  258.3 4.6 %collective-permute-done.8 = bf16[4096,16]{0,1:T(8,128)(2,1)S(1)} collective-permute-done((bf16[4096,16]{0,1:T(8,128)(2,1)S(1)}, bf16[4096,16]{0,1:T(8,128)(2,1)S(1)}, u32[]{:S(2)}, u32[]{:S(2)}) %collective-permute-start.8) | collective-permute-done | bytes 131104 | tf_op jit(solution)/shard_map/ppermute | solution.py:22
  262.9 14.2 %all_to_all.11 = bf16[16,256,16]{1,2,0:T(8,128)(2,1)S(1)} all-to-all(bf16[16,256,16]{1,2,0:T(8,128)(2,1)S(1)} %bitcast.1066), channel_id=1, replica_groups=mesh['wide_0'=4,'wide_1'=8,'narrow_0'=8,'narrow_1'=2] {'narrow_0','narro..., dimensions={0} | all-to-all | bytes 262144 | tf_op jit(solution)/shard_map/all_to_all | solution.py:75
  277.2 0.6 convert_reduce_fusion
  (27 shorter events, 0.6 us)
Async XLA Ops:
  0.6 5.3 %collective-permute-start = (bf16[16,256]{1,0:T(8,128)(2,1)}, bf16[16,256]{1,0:T(8,128)(2,1)S(1)}, u32[]{:S(2)}, u32[]{:S(2)}) collective-permute-start(bf16[16,256]{1,0:T(8,128)(2,1)} %param.5), channel_id=1, source_target_pairs={{0,16},{16,0},{32,48},{48,32},{64,80},{80,64},{96,112},{112,96},{1... | collective-permute-start | bytes 24584 | tf_op jit(solution)/shard_map/ppermute | solution.py:22
  6.7 5.5 %collective-permute-start.1 = (bf16[32,256]{1,0:T(8,128)(2,1)S(1)}, bf16[32,256]{1,0:T(8,128)(2,1)S(1)}, u32[]{:S(2)}, u32[]{:S(2)}) collective-permute-start(bf16[32,256]{1,0:T(8,128)(2,1)S(1)} %maximum_select_fusion.3), channel_id=1, source_target_pairs={{0,32},{32,0},{16,48},{48,16},{64,96},{96,64},{80,112},{112,80},{1... | collective-permute-start | bytes 49160 | tf_op jit(solution)/shard_map/ppermute | solution.py:22
  12.2 8.8 %collective-permute-start.2 = (bf16[64,256]{1,0:T(8,128)(2,1)S(1)}, bf16[64,256]{1,0:T(8,128)(2,1)S(1)}, u32[]{:S(2)}, u32[]{:S(2)}) collective-permute-start(bf16[64,256]{1,0:T(8,128)(2,1)S(1)} %maximum_select_fusion.2), channel_id=1, source_target_pairs={{0,64},{64,0},{16,80},{80,16},{32,96},{96,32},{48,112},{112,48},{1... | collective-permute-start | bytes 98312 | tf_op jit(solution)/shard_map/ppermute | solution.py:22
  21.0 5.0 %collective-permute-start.3 = (bf16[128,256]{1,0:T(8,128)(2,1)S(1)}, bf16[128,256]{1,0:T(8,128)(2,1)S(1)}, u32[]{:S(2)}, u32[]{:S(2)}) collective-permute-start(bf16[128,256]{1,0:T(8,128)(2,1)S(1)} %maximum_select_fusion.1), channel_id=1, source_target_pairs={{0,128},{128,0},{16,144},{144,16},{32,160},{160,32},{48,176},{176,... | collective-permute-start | bytes 196616 | tf_op jit(solution)/shard_map/ppermute | solution.py:22
  26.2 66.7 %copy-start = (bf16[4096,592]{0,1:T(8,128)(2,1)S(1)}, bf16[4096,592]{0,1:T(8,128)(2,1)}, u32[]{:S(2)}) copy-start(bf16[4096,592]{0,1:T(8,128)(2,1)} %param.6) | copy-start | bytes 14548996
  92.9 6.1 %copy-start.1 = (f32[256]{0:T(256)S(1)}, f32[256]{0:T(256)}, u32[]{:S(2)}) copy-start(f32[256]{0:T(256)} %param.8) | copy-start | bytes 3076
  94.3 18.1 %collective-permute-start.4 = (f32[256,592]{0,1:T(8,128)S(1)}, f32[256,592]{0,1:T(8,128)S(1)}, u32[]{:S(2)}, u32[]{:S(2)}) collective-permute-start(f32[256,592]{0,1:T(8,128)S(1)} %fusion.213), channel_id=1, source_target_pairs={{0,256},{256,0},{16,272},{272,16},{32,288},{288,32},{48,304},{304,... | collective-permute-start | bytes 1818632 | tf_op jit(solution)/shard_map/ppermute | solution.py:22
  99.0 78.7 %copy-start.4 = (s32[256]{0:T(256)S(1)}, s32[256]{0:T(256)}, u32[]{:S(2)}) copy-start(s32[256]{0:T(256)} %param.7) | copy-start | bytes 3076
  99.0 78.7 %copy-start.5 = (f32[256]{0:T(256)S(1)}, f32[256]{0:T(256)}, u32[]{:S(2)}) copy-start(f32[256]{0:T(256)} %param.9) | copy-start | bytes 3076
  177.7 4.6 %copy-start.2 = (f32[256]{0:T(256)}, f32[256]{0:T(256)S(1)}, u32[]{:S(2)}) copy-start(f32[256]{0:T(256)S(1)} %get-tuple-element.6) | copy-start | bytes 3076
  177.7 4.6 %copy-start.3 = (f32[256]{0:T(256)}, f32[256]{0:T(256)S(1)}, u32[]{:S(2)}) copy-start(f32[256]{0:T(256)S(1)} %get-tuple-element.7) | copy-start | bytes 3076
  182.6 26.3 %collective-permute-start.5 = (bf16[4096,128]{0,1:T(8,128)(2,1)S(1)}, bf16[4096,128]{0,1:T(8,128)(2,1)S(1)}, u32[]{:S(2)}, u32[]{:S(2)}) collective-permute-start(bf16[4096,128]{0,1:T(8,128)(2,1)S(1)} %select_convert_fusion), channel_id=1, source_target_pairs={{0,128},{128,0},{16,144},{144,16},{32,160},{160,32},{48,176},{176,... | collective-permute-start | bytes 3145736 | tf_op jit(solution)/shard_map/ppermute | solution.py:22
  209.3 25.2 %collective-permute-start.6 = (bf16[4096,64]{0,1:T(8,128)(2,1)S(1)}, bf16[4096,64]{0,1:T(8,128)(2,1)S(1)}, u32[]{:S(2)}, u32[]{:S(2)}) collective-permute-start(bf16[4096,64]{0,1:T(8,128)(2,1)S(1)} %select_convert_fusion.1), channel_id=1, source_target_pairs={{0,64},{64,0},{16,80},{80,16},{32,96},{96,32},{48,112},{112,48},{1... | collective-permute-start | bytes 1572872 | tf_op jit(solution)/shard_map/ppermute | solution.py:22
  234.8 21.5 %collective-permute-start.7 = (bf16[4096,32]{0,1:T(8,128)(2,1)S(1)}, bf16[4096,32]{0,1:T(8,128)(2,1)S(1)}, u32[]{:S(2)}, u32[]{:S(2)}) collective-permute-start(bf16[4096,32]{0,1:T(8,128)(2,1)S(1)} %select_convert_fusion.3), channel_id=1, source_target_pairs={{0,32},{32,0},{16,48},{48,16},{64,96},{96,64},{80,112},{112,80},{1... | collective-permute-start | bytes 786440 | tf_op jit(solution)/shard_map/ppermute | solution.py:22
  256.4 6.5 %collective-permute-start.8 = (bf16[4096,16]{0,1:T(8,128)(2,1)S(1)}, bf16[4096,16]{0,1:T(8,128)(2,1)S(1)}, u32[]{:S(2)}, u32[]{:S(2)}) collective-permute-start(bf16[4096,16]{0,1:T(8,128)(2,1)S(1)} %select_convert_fusion.5), channel_id=1, source_target_pairs={{0,16},{16,0},{32,48},{48,32},{64,80},{80,64},{96,112},{112,96},{1... | collective-permute-start | bytes 393224 | tf_op jit(solution)/shard_map/ppermute | solution.py:22
where the time goes:
time: 278 us
  blocking collectives  145 us (52%)
  waiting for transfers between devices  77.6 us (28%)
  starting transfers between devices  44.3 us (16%)
  matrix products  5.99 us (2%)
  other arithmetic  3.26 us (1%)
    ppermute x9, waiting for transfers between devices, partner(): return lax.ppermute(block, axis, route)  77.6 us
    all_to_all x1, blocking collectives, copy_for_each(): lax.all_to_all(jnp.broadcast_to(shard[None], (size, *shard.shape)), axis,...  66.5 us
    all_gather x4, blocking collectives, all_in_one(): both, at, found = (lax.all_gather(jnp.concatenate(lines), axis), 0, {})  64.4 us
    ppermute x9, starting transfers between devices, partner(): return lax.ppermute(block, axis, route)  44.3 us
    all_to_all x1, blocking collectives, summed_on_arrival(): parts = lax.all_to_all(in_blocks(shard, dim, size), axis, 0, 0, tiled=True)  14.2 us
  transfers between devices with their start and end apart: 9, of which 9 were waited for; matrix products, arithmetic and copies ran while one was open for 0% of the time, Pallas kernels for 0%

commit v1 on v0

v1 whole, which is shorter than its diff:
```python
import jax
import jax.numpy as jnp
from jax import lax
from jax.experimental import pallas as pl
from jax.experimental.pallas import tpu as pltpu
from jax.sharding import Mesh
from jax.sharding import PartitionSpec as P

HEAD, XLO, Y, Z, CORE = "head", "xlo", "y", "z", "core"
CHIPS = (XLO, Y, Z)
NARROW = (Z, CORE)
WIDE = (HEAD, XLO, Y)

BETA = 0.2
SWAP = [(0, 1), (1, 0)]
LANES = 128
STEP = 16
f32 = jnp.float32
bf16 = jnp.bfloat16
VMEM = pl.BlockSpec(memory_space=pltpu.VMEM)
SMEM = pl.BlockSpec(memory_space=pltpu.SMEM)
PARAMS = pltpu.CompilerParams(vmem_limit_bytes=40 << 20)


def logits_kernel(place, mine, other, w_mine, w_other, kept, sent, total):
    step = pl.program_id(0)
    depth = pl.num_programs(0)
    contract = (((1,), (1,)), ((), ()))
    rows = total.shape[1]
    part = lax.dot_general(
        w_mine[...], mine[...].reshape(rows, -1), contract, preferred_element_type=f32
    ) + lax.dot_general(
        w_other[...], other[...].reshape(rows, -1), contract, preferred_element_type=f32
    )

    @pl.when(step == 0)
    def _():
        total[...] = part

    @pl.when(step > 0)
    def _():
        total[...] += part

    half = rows // 2

    @pl.when((step == depth - 1) & (place[0] == 0))
    def _():
        kept[...] = total[:, :half]
        sent[...] = total[:, half:]

    @pl.when((step == depth - 1) & (place[0] == 1))
    def _():
        kept[...] = total[:, half:]
        sent[...] = total[:, :half]


def logits_of(place, mine, other, weights):
    blocks, depth, rows, width = mine.shape
    columns = weights.shape[0]
    row_total = blocks * rows
    hidden_spec = pl.BlockSpec((blocks, 1, rows, width), lambda z, s: (0, z, 0, 0))
    out = jax.ShapeDtypeStruct((columns, row_total // 2), f32)
    out_spec = pl.BlockSpec(out.shape, lambda z, s: (0, 0))
    return pl.pallas_call(
        logits_kernel,
        grid_spec=pltpu.PrefetchScalarGridSpec(
            num_scalar_prefetch=1,
            grid=(depth,),
            in_specs=[
                hidden_spec,
                hidden_spec,
                pl.BlockSpec((columns, width), lambda z, s: (0, 2 * z + s[1])),
                pl.BlockSpec((columns, width), lambda z, s: (0, 2 * z + 1 - s[1])),
            ],
            out_specs=[out_spec, out_spec],
            scratch_shapes=[pltpu.VMEM((columns, row_total), f32)],
        ),
        out_shape=[out, out],
        compiler_params=PARAMS,
        name="logits",
    )(place, mine, other, weights, weights)


def stats_kernel(place, kept, got, out):
    def write(policy, refer):
        mixed = (1.0 - BETA) * policy + BETA * refer
        top = jnp.max(policy, 0, keepdims=True)
        mixed_top = jnp.max(mixed, 0, keepdims=True)
        weight = jnp.exp(policy - top)
        total = jnp.sum(weight, 0, keepdims=True)
        cross = jnp.sum(weight * (policy - mixed), 0, keepdims=True) / total
        mixed_total = jnp.sum(jnp.exp(mixed - mixed_top), 0, keepdims=True)
        lines = (top + jnp.log(total), cross, mixed_top + jnp.log(mixed_total))
        out[...] = spread(lines, out.shape)

    @pl.when(place[0] == 0)
    def _():
        write(kept[...], got[...])

    @pl.when(place[0] == 1)
    def _():
        write(got[...], kept[...])


def spread(lines, shape):
    count, height, width = shape
    tail = jnp.zeros((height - len(lines), width), f32)
    tile = jnp.concatenate([*lines, tail], 0)
    return jnp.broadcast_to(tile[None], shape)


def merged(tiles):
    top = jnp.max(tiles, 0)
    weight = jnp.exp(tiles - top[None])
    total = jnp.sum(weight, 0)
    lse = top + jnp.log(total)
    cross = jnp.sum(weight[:, 0:1] * tiles[:, 1:2], 0) / total[0:1]
    return lse[0:1], cross, lse[2:3]


def merge_kernel(tiles, out):
    out[...] = spread(merged(tiles[...]), out.shape)


def final_kernel(tiles, out):
    count = tiles.shape[0] // 2
    half = tiles.shape[2]
    for k in range(2):
        policy_lse, cross, mixture_lse = merged(tiles[k * count : (k + 1) * count])
        divergence = cross - policy_lse + mixture_lse
        lines = (policy_lse, divergence, mixture_lse)
        out[:, k * half : (k + 1) * half] = spread(lines, (1, 8, half))[0]


def grads_kernel(
    place, kept, got, sent, late, final, ids, kl_weight, advantage, w_mine, w_other,
    kept_out, sent_out, flat, turned,
):
    columns, half = kept.shape
    padded = flat.shape[0]

    def fill(low, high, policy_head):
        for k, (own_ref, partner_ref) in enumerate((low, high)):
            at = slice(k * half, (k + 1) * half)
            policy_lse, divergence, mixture_lse = (final[i : i + 1, at] for i in range(3))
            kl = kl_weight[:, at]
            adv = advantage[:, at]
            token = ids[:, at] - place[2]

            def rows(i, _, own_ref=own_ref, partner_ref=partner_ref):
                start = pl.multiple_of(i * STEP, STEP)
                own, partner = own_ref[pl.ds(start, STEP)], partner_ref[pl.ds(start, STEP)]
                policy, refer = (own, partner) if policy_head else (partner, own)
                mixed = (1.0 - BETA) * policy + BETA * refer
                policy_prob = jnp.exp(policy - policy_lse)
                mixture_prob = jnp.exp(mixed - mixture_lse)
                shift = mixture_prob - policy_prob
                if policy_head:
                    gap = policy - policy_lse - mixed + mixture_lse
                    column = start + lax.broadcasted_iota(jnp.int32, (STEP, half), 0)
                    chosen = (token == column).astype(f32)
                    grad = kl * (
                        policy_prob * (gap - divergence) + (1.0 - BETA) * shift
                    ) - adv * (chosen - policy_prob)
                else:
                    grad = BETA * kl * shift
                flat[pl.ds(start, STEP), at] = grad
                return _

            lax.fori_loop(0, columns // STEP, rows, None, unroll=True)
        flat[columns:, :] = jnp.zeros((padded - columns, flat.shape[1]), f32)
        for start in range(0, padded, LANES):
            turned[:, start : start + LANES] = flat[start : start + LANES, :].T.astype(bf16)

    @pl.when((pl.program_id(0) == 0) & (place[0] == 0))
    def _():
        fill((kept, got), (sent, late), True)

    @pl.when((pl.program_id(0) == 0) & (place[0] == 1))
    def _():
        fill((sent, late), (kept, got), False)

    grad = turned[:, :columns]
    contract = (((1,), (0,)), ((), ()))
    mine = lax.dot_general(grad, w_mine[...], contract, preferred_element_type=f32)
    kept_out[...] = mine.reshape(kept_out.shape)
    other = lax.dot_general(grad, w_other[...], contract, preferred_element_type=f32)
    sent_out[...] = other.astype(bf16).reshape(sent_out.shape)


def grads_of(place, kept, got, sent, late, final, ids, kl_weight, advantage, weights, shape):
    blocks, depth, rows, width = shape
    columns = weights.shape[0]
    row_total = blocks * rows
    whole = lambda a: pl.BlockSpec(a.shape, lambda z, s: (0, 0))
    spec = pl.BlockSpec((blocks, 1, rows, width), lambda z, s: (0, z, 0, 0))
    small = [kept, got, sent, late, final, ids, kl_weight, advantage]
    padded = -(-columns // LANES) * LANES
    return pl.pallas_call(
        grads_kernel,
        grid_spec=pltpu.PrefetchScalarGridSpec(
            num_scalar_prefetch=1,
            grid=(depth,),
            in_specs=[
                *(whole(a) for a in small),
                pl.BlockSpec((columns, width), lambda z, s: (0, 2 * z + s[1])),
                pl.BlockSpec((columns, width), lambda z, s: (0, 2 * z + 1 - s[1])),
            ],
            out_specs=[spec, spec],
            scratch_shapes=[
                pltpu.VMEM((padded, row_total), f32),
                pltpu.VMEM((row_total, padded), bf16),
            ],
        ),
        out_shape=[jax.ShapeDtypeStruct(shape, f32), jax.ShapeDtypeStruct(shape, bf16)],
        compiler_params=PARAMS,
        name="grads",
    )(place, *small, weights, weights)


def on_core(kernel, shape, specs, name):
    return pl.pallas_call(
        kernel,
        in_specs=specs,
        out_specs=VMEM,
        out_shape=jax.ShapeDtypeStruct(shape, f32),
        compiler_params=PARAMS,
        name=name,
    )


def body(hidden, head_weights, token_ids, kl_weight, advantage):
    rows, width = hidden.shape
    columns = head_weights.shape[1]
    row_blocks = lax.axis_size((XLO, Y))
    depth = lax.axis_size(Z)
    chips = row_blocks * depth
    row_total = rows * row_blocks
    half = row_total // 2
    col_start = lax.axis_index((XLO, Y, Z, CORE)) * columns
    place = jnp.stack([lax.axis_index(HEAD), lax.axis_index(CORE), col_start]).astype(jnp.int32)
    weights = head_weights.T

    mine = lax.all_to_all(
        jnp.broadcast_to(hidden[None], (chips, rows, width)), CHIPS, 0, 0, tiled=True
    )
    other = lax.ppermute(mine, CORE, SWAP)
    shape = (row_blocks, depth, rows, width)
    kept, sent = logits_of(place, mine.reshape(shape), other.reshape(shape), weights)

    got = lax.ppermute(sent, HEAD, SWAP)
    narrow, wide = lax.axis_size(NARROW), lax.axis_size(WIDE)
    stats = on_core(stats_kernel, (narrow, 8, half), [SMEM, VMEM, VMEM], "stats")(place, kept, got)
    kept_late, stats = lax.optimization_barrier((kept, stats))
    late = lax.ppermute(kept_late, HEAD, SWAP)
    stats = lax.all_to_all(stats, NARROW, 0, 0, tiled=True)
    stats = on_core(merge_kernel, (wide, 8, half), [VMEM], "merge")(stats)
    stats = lax.all_to_all(stats, WIDE, 0, 0, tiled=True)
    final = on_core(final_kernel, (8, row_total), [VMEM], "final")(stats)

    line = lambda a: a.reshape(1, row_total)
    kept_part, sent_part = grads_of(
        place, kept, got, sent, late, final, line(token_ids), line(kl_weight), line(advantage),
        weights, shape,
    )
    back = lax.ppermute(sent_part, CORE, SWAP)
    pair_sum = (kept_part + back.astype(f32)).astype(bf16).reshape(chips, rows, width)
    arrived = lax.all_to_all(pair_sum, CHIPS, 0, 0, tiled=True)
    hidden_grad = jnp.sum(arrived.astype(f32), 0).T
    return (hidden_grad, final[2], final[1])


def solution(mesh):
    finer = Mesh(mesh.devices.reshape(2, 2, 8, 8, 2), (HEAD, XLO, Y, Z, CORE))
    return jax.shard_map(
        body,
        mesh=finer,
        in_specs=(P(WIDE, NARROW), P(None, (*WIDE, *NARROW)), P(), P(), P()),
        out_specs=(P(NARROW, WIDE), P(), P()),
        check_vma=False,
    )
```

time: 278 us -> 158 us (0.57)
  blocking collectives: 145 us -> 62.1 us
  waiting for transfers between devices: 77.6 us -> 44.8 us
  starting transfers between devices: 44.3 us -> 29.1 us
  Pallas kernels: 0 us -> 11.8 us
  matrix products: 5.99 us -> 0 us
  local copies, waits for them, and re-layouts: 0.45 us -> 6.09 us
    ppermute x9 -> x4, waiting for transfers between devices: 77.6 us -> 11.8 us  [the longest x1 7.39 us: body(): got = lax.ppermute(sent, HEAD, SWAP)]
    all_gather x4 -> x0, blocking collectives: 64.4 us -> none  [all_in_one(): both, at, found = (lax.all_gather(jnp.concatenate(lines), axis), 0, {})]
    all_to_all x0 -> x2, waiting for transfers between devices: none -> 33 us  [the longest x1 29.5 us: body(): arrived = lax.all_to_all(pair_sum, CHIPS, 0, 0, tiled=True)]
    ppermute x9 -> x4, starting transfers between devices: 44.3 us -> 18.4 us  [the longest x1 5.61 us: body(): other = lax.ppermute(mine, CORE, SWAP)]
    all_to_all x2, blocking collectives: 80.7 us -> 62.1 us  [the longest x1 48.3 us: body(): lax.all_to_all(jnp.broadcast_to(hidden[None], (chips, rows, width)), CHIP...]
    pallas_call x0 -> x5, Pallas kernels: none -> 11.8 us  [the longest x1 5.25 us: grads_of(): pl.pallas_call(grads_kernel, grid_spec=pltpu.PrefetchScalarGridSpec(num_s...]
    all_to_all x0 -> x2, starting transfers between devices: none -> 10.7 us  [the longest x1 6.19 us: body(): arrived = lax.all_to_all(pair_sum, CHIPS, 0, 0, tiled=True)]
    dot_general x2 -> x0, matrix products: 5.99 us -> none  [the longest x1 4.58 us: body(): lax.dot_general(head_weights, own_grad, contract, preferred_element_type=...]
  transfers between devices with their start and end apart: 9 -> 6, of which waited for: 9 -> 5; matrix products, arithmetic and copies ran while one was open for 0% -> 0% of each run, Pallas kernels for 0% -> 0%
where the time goes in v1:
time: 158 us; the launch traced here: 157 us
  blocking collectives  62.1 us (39%)
  waiting for transfers between devices  44.8 us (28%)
  starting transfers between devices  29.1 us (18%)
  Pallas kernels  11.8 us (7%)
  local copies, waits for them, and re-layouts  6.09 us (4%)
  other arithmetic  2.24 us (1%)
    all_to_all x1, blocking collectives, body(): lax.all_to_all(jnp.broadcast_to(hidden[None], (chips, rows, width)), CHIP...  48.3 us
    all_to_all x1, waiting for transfers between devices, body(): arrived = lax.all_to_all(pair_sum, CHIPS, 0, 0, tiled=True)  29.5 us
    all_to_all x1, blocking collectives, body(): stats = lax.all_to_all(stats, WIDE, 0, 0, tiled=True)  13.8 us
    ppermute x1, waiting for transfers between devices, body(): got = lax.ppermute(sent, HEAD, SWAP)  7.39 us
    all_to_all x1, starting transfers between devices, body(): arrived = lax.all_to_all(pair_sum, CHIPS, 0, 0, tiled=True)  6.19 us
    ppermute x1, starting transfers between devices, body(): other = lax.ppermute(mine, CORE, SWAP)  5.61 us
    pallas_call x1, Pallas kernels, grads_of(): pl.pallas_call(grads_kernel, grid_spec=pltpu.PrefetchScalarGridSpec(num_s...  5.25 us
    pallas_call x1, Pallas kernels, logits_of(): pl.pallas_call(logits_kernel, grid_spec=pltpu.PrefetchScalarGridSpec(num_...  5.03 us
  transfers between devices with their start and end apart: 6, of which 5 were waited for; matrix products, arithmetic and copies ran while one was open for 0% of the time, Pallas kernels for 0%

profile of v1, /device:TPU:1, one launch (start us, length us, event | category | flops | bytes accessed | tf_op | source)
XLA Modules:
  0.0 156.8 jit_solution(16220332000125373029)
XLA Ops:
  0.6 0.8 broadcast_in_dim.2
  1.4 48.3 %all_to_all.20 = bf16[128,16,256]{2,1,0:T(8,128)(2,1)S(1)} all-to-all(bf16[128,16,256]{2,1,0:T(8,128)(2,1)S(1)} %broadcast_in_dim.2), channel_id=1, replica_groups=mesh['head'=2,'xlo'=2,'y'=8,'z'=8,'core'=2] {'xlo','y','z'}, dimensions={0} | all-to-all | bytes 2097152 | tf_op jit(solution)/shard_map/all_to_all | solution.py:244
  49.7 5.6 %collective-permute-start = (bf16[128,16,256]{2,1,0:T(8,128)(2,1)S(1)}, bf16[128,16,256]{2,1,0:T(8,128)(2,1)S(1)}, u32[]{:S(2)}, u32[]{:S(2)}) collective-permute-start(bf16[128,16,256]{2,1,0:T(8,128)(2,1)S(1)} %all_to_all.20), channel_id=1, source_target_pairs={{0,1},{1,0},{2,3},{3,2},{4,5},{5,4},{6,7},{7,6},{8,9},{9,8},{10,11... | collective-permute-start | bytes 3145736 | tf_op jit(solution)/shard_map/ppermute | solution.py:247
  55.3 0.1 pad_add_fusion.place
  55.4 2.2 %collective-permute-done = bf16[128,16,256]{2,1,0:T(8,128)(2,1)S(1)} collective-permute-done((bf16[128,16,256]{2,1,0:T(8,128)(2,1)S(1)}, bf16[128,16,256]{2,1,0:T(8,128)(2,1)S(1)}, u32[]{:S(2)}, u32[]{:S(2)}) %collective-permute-start) | collective-permute-done | bytes 1048608 | tf_op jit(solution)/shard_map/ppermute | solution.py:247
  57.6 0.0 copy-start
  57.6 2.4 %copy-done = bf16[4096,592]{0,1:T(8,128)(2,1)S(1)} copy-done((bf16[4096,592]{0,1:T(8,128)(2,1)S(1)}, bf16[4096,592]{0,1:T(8,128)(2,1)}, u32[]{:S(2)}) %copy-start) | copy-done | bytes 4849688
  60.0 0.0 copy-start.2
  60.0 0.0 copy-start.3
  60.0 0.0 copy-start.4
  60.0 5.0 %logits.1 = (f32[592,128]{1,0:T(8,128)S(1)}, f32[592,128]{1,0:T(8,128)S(1)}) custom-call(s32[3]{0:T(128)S(1)} %pad_add_fusion.place, bf16[16,8,16,256]{3,2,1,0:T(8,128)(2,1)S(1)} %bitcast.17, bf16[16,8,16,256]{3,2,1,0:T(8,128)(2,1)S(1)} %bitcast.18, bf16[592,4096]{1,0:T(8,128)(2,1)S(1)} %bitcast.13, bf16[592,4096]{1,0:T(8,128)(2,1)S(1)} %bitcast.14), custom_call_target="tpu_custom_call" | custom-call | tf_op jit(solution)/shard_map/logits/pallas_call | solution.py:64
  65.0 4.4 %collective-permute-start.1 = (f32[592,128]{1,0:T(8,128)S(1)}, f32[592,128]{1,0:T(8,128)S(1)}, u32[]{:S(2)}, u32[]{:S(2)}) collective-permute-start(f32[592,128]{1,0:T(8,128)S(1)} %get-tuple-element.10.sent), channel_id=1, source_target_pairs={{0,256},{256,0},{1,257},{257,1},{2,258},{258,2},{3,259},{259,3},{4... | collective-permute-start | bytes 909320 | tf_op jit(solution)/shard_map/ppermute | solution.py:251
  69.4 7.4 %collective-permute-done.1.got = f32[592,128]{1,0:T(8,128)S(1)} collective-permute-done((f32[592,128]{1,0:T(8,128)S(1)}, f32[592,128]{1,0:T(8,128)S(1)}, u32[]{:S(2)}, u32[]{:S(2)}) %collective-permute-start.1) | collective-permute-done | bytes 303136 | tf_op jit(solution)/shard_map/ppermute | solution.py:251
  76.8 1.4 stats.1
  78.2 4.5 %all-to-all-start.1 = ((f32[16,8,128]{2,1,0:T(8,128)}), f32[16,8,128]{2,1,0:T(8,128)S(1)}, u32[]{:S(2)}, u32[]{:S(2)}) async-start(f32[16,8,128]{2,1,0:T(8,128)} %stats.1), calls=%async_computation.1 | async-start | bytes 131072 | tf_op jit(solution)/shard_map/all_to_all | solution.py:256
  82.7 4.4 %collective-permute-start.2 = (f32[592,128]{1,0:T(8,128)S(1)}, f32[592,128]{1,0:T(8,128)S(1)}, u32[]{:S(2)}, u32[]{:S(2)}) collective-permute-start(f32[592,128]{1,0:T(8,128)S(1)} %get-tuple-element.11.kept), channel_id=1, source_target_pairs={{0,256},{256,0},{1,257},{257,1},{2,258},{258,2},{3,259},{259,3},{4... | collective-permute-start | bytes 909320 | tf_op jit(solution)/shard_map/ppermute | solution.py:255
  87.1 3.5 %all-to-all-done.1.tiles = f32[16,8,128]{2,1,0:T(8,128)S(1)} async-done(((f32[16,8,128]{2,1,0:T(8,128)}), f32[16,8,128]{2,1,0:T(8,128)S(1)}, u32[]{:S(2)}, u32[]{:S(2)}) %all-to-all-start.1) | async-done | bytes 65568 | tf_op jit(solution)/shard_map/all_to_all | solution.py:256
  90.6 13.8 %all_to_all.21.tiles = f32[32,8,128]{2,1,0:T(8,128)S(1)} all-to-all(f32[32,8,128]{2,1,0:T(8,128)S(1)} %merge.1), channel_id=1, replica_groups=mesh['head'=2,'xlo'=2,'y'=8,'z'=8,'core'=2] {'head','xlo','y'}, dimensions={0} | all-to-all | bytes 262144 | tf_op jit(solution)/shard_map/all_to_all | solution.py:258
  104.4 0.1 final.1
  104.4 0.0 collective-permute-done.2.late
  104.5 0.0 copy-done.2
  104.5 0.0 copy-done.3
  104.5 0.0 copy-done.4
  104.5 0.0 copy-start.1
  104.5 2.4 %copy-done.1 = bf16[4096,592]{0,1:T(8,128)(2,1)S(1)} copy-done((bf16[4096,592]{0,1:T(8,128)(2,1)S(1)}, bf16[4096,592]{0,1:T(8,128)(2,1)}, u32[]{:S(2)}) %copy-start.1) | copy-done | bytes 4849688
  106.9 5.2 %grads.1 = (f32[16,8,16,256]{3,2,1,0:T(8,128)S(1)}, bf16[16,8,16,256]{3,2,1,0:T(8,128)(2,1)S(1)}) custom-call(s32[3]{0:T(128)S(1)} %pad_add_fusion.place, f32[592,128]{1,0:T(8,128)S(1)} %get-tuple-element.11.kept, f32[592,128]{1,0:T(8,128)S(1)} %collective-permute-done.1.got, f32[592,128]{1,0:T(8,128)S(1)} %get-tuple-element.10.sent, ...), custom_call_target="tpu_custom_call" | custom-call | tf_op jit(solution)/shard_map/grads/pallas_call | solution.py:199
  112.1 4.0 %collective-permute-start.3 = (bf16[16,8,16,256]{3,2,1,0:T(8,128)(2,1)S(1)}, bf16[16,8,16,256]{3,2,1,0:T(8,128)(2,1)S(1)}, u32[]{:S(2)}, u32[]{:S(2)}) collective-permute-start(bf16[16,8,16,256]{3,2,1,0:T(8,128)(2,1)S(1)} %get-tuple-element.14), channel_id=1, source_target_pairs={{0,1},{1,0},{2,3},{3,2},{4,5},{5,4},{6,7},{7,6},{8,9},{9,8},{10,11... | collective-permute-start | bytes 3145736 | tf_op jit(solution)/shard_map/ppermute | solution.py:266
  116.1 2.3 %collective-permute-done.3 = bf16[16,8,16,256]{3,2,1,0:T(8,128)(2,1)S(1)} collective-permute-done((bf16[16,8,16,256]{3,2,1,0:T(8,128)(2,1)S(1)}, bf16[16,8,16,256]{3,2,1,0:T(8,128)(2,1)S(1)}, u32[]{:S(2)}, u32[]{:S(2)}) %collective-permute-start.3) | collective-permute-done | bytes 1048608 | tf_op jit(solution)/shard_map/ppermute | solution.py:266
  118.4 1.4 add_convert_fusion
  119.8 6.2 %all-to-all-start.3 = ((bf16[128,16,256]{2,1,0:T(8,128)(2,1)}), bf16[128,16,256]{2,1,0:T(8,128)(2,1)S(1)}, u32[]{:S(2)}, u32[]{:S(2)}) async-start(bf16[128,16,256]{2,1,0:T(8,128)(2,1)} %bitcast.9), calls=%async_computation.3 | async-start | bytes 2097152 | tf_op jit(solution)/shard_map/all_to_all | solution.py:268
  126.0 0.6 fusion
  126.5 29.5 %all-to-all-done.3 = bf16[128,16,256]{2,1,0:T(8,128)(2,1)S(1)} async-done(((bf16[128,16,256]{2,1,0:T(8,128)(2,1)}), bf16[128,16,256]{2,1,0:T(8,128)(2,1)S(1)}, u32[]{:S(2)}, u32[]{:S(2)}) %all-to-all-start.3) | async-done | bytes 1048608 | tf_op jit(solution)/shard_map/all_to_all | solution.py:268
  156.0 0.8 convert_reduce_fusion
  (1 shorter events, 0.0 us)
Async XLA Ops:
  49.7 7.9 %collective-permute-start = (bf16[128,16,256]{2,1,0:T(8,128)(2,1)S(1)}, bf16[128,16,256]{2,1,0:T(8,128)(2,1)S(1)}, u32[]{:S(2)}, u32[]{:S(2)}) collective-permute-start(bf16[128,16,256]{2,1,0:T(8,128)(2,1)S(1)} %all_to_all.20), channel_id=1, source_target_pairs={{0,1},{1,0},{2,3},{3,2},{4,5},{5,4},{6,7},{7,6},{8,9},{9,8},{10,11... | collective-permute-start | bytes 3145736 | tf_op jit(solution)/shard_map/ppermute | solution.py:247
  57.6 2.4 %copy-start = (bf16[4096,592]{0,1:T(8,128)(2,1)S(1)}, bf16[4096,592]{0,1:T(8,128)(2,1)}, u32[]{:S(2)}) copy-start(bf16[4096,592]{0,1:T(8,128)(2,1)} %param.6) | copy-start | bytes 14548996
  60.0 44.5 %copy-start.2 = (s32[256]{0:T(256)S(1)}, s32[256]{0:T(256)}, u32[]{:S(2)}) copy-start(s32[256]{0:T(256)} %param.7) | copy-start | bytes 3076
  60.0 44.5 %copy-start.3 = (f32[256]{0:T(256)S(1)}, f32[256]{0:T(256)}, u32[]{:S(2)}) copy-start(f32[256]{0:T(256)} %param.8) | copy-start | bytes 3076
  60.0 44.5 %copy-start.4 = (f32[256]{0:T(256)S(1)}, f32[256]{0:T(256)}, u32[]{:S(2)}) copy-start(f32[256]{0:T(256)} %param.9) | copy-start | bytes 3076
  65.0 11.8 %collective-permute-start.1 = (f32[592,128]{1,0:T(8,128)S(1)}, f32[592,128]{1,0:T(8,128)S(1)}, u32[]{:S(2)}, u32[]{:S(2)}) collective-permute-start(f32[592,128]{1,0:T(8,128)S(1)} %get-tuple-element.10.sent), channel_id=1, source_target_pairs={{0,256},{256,0},{1,257},{257,1},{2,258},{258,2},{3,259},{259,3},{4... | collective-permute-start | bytes 909320 | tf_op jit(solution)/shard_map/ppermute | solution.py:251
  78.2 12.3 %all-to-all-start.1 = ((f32[16,8,128]{2,1,0:T(8,128)}), f32[16,8,128]{2,1,0:T(8,128)S(1)}, u32[]{:S(2)}, u32[]{:S(2)}) async-start(f32[16,8,128]{2,1,0:T(8,128)} %stats.1), calls=%async_computation.1 | async-start | bytes 131072 | tf_op jit(solution)/shard_map/all_to_all | solution.py:256
  82.7 21.8 %collective-permute-start.2 = (f32[592,128]{1,0:T(8,128)S(1)}, f32[592,128]{1,0:T(8,128)S(1)}, u32[]{:S(2)}, u32[]{:S(2)}) collective-permute-start(f32[592,128]{1,0:T(8,128)S(1)} %get-tuple-element.11.kept), channel_id=1, source_target_pairs={{0,256},{256,0},{1,257},{257,1},{2,258},{258,2},{3,259},{259,3},{4... | collective-permute-start | bytes 909320 | tf_op jit(solution)/shard_map/ppermute | solution.py:255
  104.5 2.4 %copy-start.1 = (bf16[4096,592]{0,1:T(8,128)(2,1)S(1)}, bf16[4096,592]{0,1:T(8,128)(2,1)}, u32[]{:S(2)}) copy-start(bf16[4096,592]{0,1:T(8,128)(2,1)} %param.6) | copy-start | bytes 14548996
  112.1 6.3 %collective-permute-start.3 = (bf16[16,8,16,256]{3,2,1,0:T(8,128)(2,1)S(1)}, bf16[16,8,16,256]{3,2,1,0:T(8,128)(2,1)S(1)}, u32[]{:S(2)}, u32[]{:S(2)}) collective-permute-start(bf16[16,8,16,256]{3,2,1,0:T(8,128)(2,1)S(1)} %get-tuple-element.14), channel_id=1, source_target_pairs={{0,1},{1,0},{2,3},{3,2},{4,5},{5,4},{6,7},{7,6},{8,9},{9,8},{10,11... | collective-permute-start | bytes 3145736 | tf_op jit(solution)/shard_map/ppermute | solution.py:266
  119.8 36.3 %all-to-all-start.3 = ((bf16[128,16,256]{2,1,0:T(8,128)(2,1)}), bf16[128,16,256]{2,1,0:T(8,128)(2,1)S(1)}, u32[]{:S(2)}, u32[]{:S(2)}) async-start(bf16[128,16,256]{2,1,0:T(8,128)(2,1)} %bitcast.9), calls=%async_computation.3 | async-start | bytes 2097152 | tf_op jit(solution)/shard_map/all_to_all | solution.py:268

commit v2 on v1

v2 whole, which is shorter than its diff:
```python
import jax
import jax.numpy as jnp
from jax import lax
from jax.experimental import pallas as pl
from jax.experimental.pallas import tpu as pltpu
from jax.sharding import Mesh
from jax.sharding import PartitionSpec as P

HEAD, XLO, YHI, YLO, ZHI, ZLO, CORE = "head", "xlo", "yhi", "ylo", "zhi", "zlo", "core"
Y = (YHI, YLO)
Z = (ZHI, ZLO)
NARROW = (*Z, CORE)
WIDE = (HEAD, XLO, *Y)
GATHER_FAR, GATHER_NEAR = (*Y, ZHI), (XLO, ZLO)
REDUCE_NEAR, REDUCE_FAR = (YLO, ZLO), (XLO, YHI, ZHI)

BETA = 0.2
SWAP = [(0, 1), (1, 0)]
LANES = 128
STEP = 16
f32 = jnp.float32
bf16 = jnp.bfloat16
VMEM = pl.BlockSpec(memory_space=pltpu.VMEM)
HBM = pl.BlockSpec(memory_space=pltpu.HBM)
SMEM = pl.BlockSpec(memory_space=pltpu.SMEM)
WIDE_PARAMS = pltpu.CompilerParams(vmem_limit_bytes=50 << 20)
PARAMS = pltpu.CompilerParams(vmem_limit_bytes=16 << 20)


def fetches(weights, core, buffer, sems):
    depth, _, width = buffer.shape
    copies = []
    for z in range(depth):
        start = pl.multiple_of((2 * z + core) * width, width)
        copies.append(
            pltpu.make_async_copy(weights.at[:, pl.ds(start, width)], buffer.at[z], sems.at[z])
        )
        copies[z].start()
    return copies


def products(blocks, copies, buffer):
    xlo, zlo, y, zhi, rows, width = blocks.shape
    total = None
    for z, copy in enumerate(copies):
        hi, lo = z // zlo, z % zlo
        copy.wait()
        part = lax.dot_general(
            buffer[z],
            blocks[:, lo, :, hi].reshape(xlo * y * rows, width),
            (((1,), (1,)), ((), ())),
            preferred_element_type=f32,
        )
        total = part if total is None else total + part
    return total


def first_kernel(place, mine, weights, out, buffer, sems):
    out[...] = products(mine, fetches(weights, place[1], buffer, sems), buffer)


def second_kernel(place, part, other, weights, kept, sent, buffer, sems):
    copies = fetches(weights, 1 - place[1], buffer, sems)
    total = part[...] + products(other, copies, buffer)
    half = kept.shape[1]

    @pl.when(place[0] == 0)
    def _():
        kept[...] = total[:, :half]
        sent[...] = total[:, half:]

    @pl.when(place[0] == 1)
    def _():
        kept[...] = total[:, half:]
        sent[...] = total[:, :half]


def stats_kernel(place, kept, got, out):
    def write(policy, refer):
        mixed = (1.0 - BETA) * policy + BETA * refer
        top = jnp.max(policy, 0, keepdims=True)
        mixed_top = jnp.max(mixed, 0, keepdims=True)
        weight = jnp.exp(policy - top)
        total = jnp.sum(weight, 0, keepdims=True)
        cross = jnp.sum(weight * (policy - mixed), 0, keepdims=True) / total
        mixed_total = jnp.sum(jnp.exp(mixed - mixed_top), 0, keepdims=True)
        lines = (top + jnp.log(total), cross, mixed_top + jnp.log(mixed_total))
        out[...] = spread(lines, out.shape)

    @pl.when(place[0] == 0)
    def _():
        write(kept[...], got[...])

    @pl.when(place[0] == 1)
    def _():
        write(got[...], kept[...])


def spread(lines, shape):
    count, height, width = shape
    tail = jnp.zeros((height - len(lines), width), f32)
    tile = jnp.concatenate([*lines, tail], 0)
    return jnp.broadcast_to(tile[None], shape)


def merged(tiles):
    top = jnp.max(tiles, 0)
    weight = jnp.exp(tiles - top[None])
    total = jnp.sum(weight, 0)
    lse = top + jnp.log(total)
    cross = jnp.sum(weight[:, 0:1] * tiles[:, 1:2], 0) / total[0:1]
    return lse[0:1], cross, lse[2:3]


def merge_kernel(tiles, out):
    out[...] = spread(merged(tiles[...]), out.shape)


def final_kernel(tiles, out):
    count = tiles.shape[0] // 2
    half = tiles.shape[2]
    for k in range(2):
        policy_lse, cross, mixture_lse = merged(tiles[k * count : (k + 1) * count])
        divergence = cross - policy_lse + mixture_lse
        lines = (policy_lse, divergence, mixture_lse)
        out[:, k * half : (k + 1) * half] = spread(lines, (1, 8, half))[0]


def sent_kernel(
    place, kept, got, sent, late, final, ids, kl_weight, advantage, weights,
    turned, sent_out, flat, buffer, sems,
):
    copies = fetches(weights, 1 - place[1], buffer, sems)
    columns, half = kept.shape
    padded = flat.shape[0]

    def fill(low, high, policy_head):
        for k, (own_ref, partner_ref) in enumerate((low, high)):
            at = slice(k * half, (k + 1) * half)
            policy_lse, divergence, mixture_lse = (final[i : i + 1, at] for i in range(3))
            kl = kl_weight[:, at]
            adv = advantage[:, at]
            token = ids[:, at] - place[2]

            def rows(i, _, own_ref=own_ref, partner_ref=partner_ref):
                start = pl.multiple_of(i * STEP, STEP)
                own, partner = own_ref[pl.ds(start, STEP)], partner_ref[pl.ds(start, STEP)]
                policy, refer = (own, partner) if policy_head else (partner, own)
                mixed = (1.0 - BETA) * policy + BETA * refer
                policy_prob = jnp.exp(policy - policy_lse)
                mixture_prob = jnp.exp(mixed - mixture_lse)
                shift = mixture_prob - policy_prob
                if policy_head:
                    gap = policy - policy_lse - mixed + mixture_lse
                    column = start + lax.broadcasted_iota(jnp.int32, (STEP, half), 0)
                    chosen = (token == column).astype(f32)
                    grad = kl * (
                        policy_prob * (gap - divergence) + (1.0 - BETA) * shift
                    ) - adv * (chosen - policy_prob)
                else:
                    grad = BETA * kl * shift
                flat[pl.ds(start, STEP), at] = grad
                return _

            lax.fori_loop(0, columns // STEP, rows, None, unroll=True)
        flat[columns:, :] = jnp.zeros((padded - columns, flat.shape[1]), f32)
        for start in range(0, padded, LANES):
            turned[:, start : start + LANES] = flat[start : start + LANES, :].T.astype(bf16)

    @pl.when(place[0] == 0)
    def _():
        fill((kept, got), (sent, late), True)

    @pl.when(place[0] == 1)
    def _():
        fill((sent, late), (kept, got), False)

    for z, part in sums(turned, copies, buffer):
        sent_out[z] = part.astype(bf16)


def sums(turned, copies, buffer):
    grad = turned[:, : buffer.shape[1]]
    for z, copy in enumerate(copies):
        copy.wait()
        yield z, lax.dot_general(
            grad, buffer[z], (((1,), (0,)), ((), ())), preferred_element_type=f32
        )


def pair_kernel(place, turned, back, weights, out, buffer, sems):
    ylo, zlo, xlo, yhi, zhi, rows, width = out.shape
    copies = fetches(weights, place[1], buffer, sems)
    for z, part in sums(turned, copies, buffer):
        whole = (part + back[z].astype(f32)).astype(bf16)
        whole = whole.reshape(xlo, yhi, ylo, rows, width)
        for lo in range(ylo):
            out[lo, z % zlo, :, :, z // zlo] = whole[:, :, lo]


def on_core(kernel, out_shape, count, name, scalars=True, scratch=(), hbm=0):
    return pl.pallas_call(
        kernel,
        in_specs=[SMEM] * scalars + [VMEM] * count + [HBM] * hbm,
        out_specs=jax.tree.map(lambda _: VMEM, out_shape),
        out_shape=out_shape,
        scratch_shapes=scratch,
        compiler_params=WIDE_PARAMS if hbm else PARAMS,
        name=name,
    )


def array(shape, dtype=f32):
    return jax.ShapeDtypeStruct(shape, dtype)


def copies(block, axes):
    count = lax.axis_size(axes)
    return lax.all_to_all(
        jnp.broadcast_to(block[None], (count, *block.shape)), axes, 0, 0, tiled=True
    )


def exchange_sum(parts, axes):
    return jnp.sum(lax.all_to_all(parts, axes, 0, 0, tiled=True).astype(f32), 0)


def body(hidden, head_weights, token_ids, kl_weight, advantage):
    rows, width = hidden.shape
    columns = head_weights.shape[1]
    xlo, yhi, ylo, zhi, zlo = (lax.axis_size(a) for a in (XLO, YHI, YLO, ZHI, ZLO))
    depth = zhi * zlo
    row_total = rows * xlo * yhi * ylo
    half = row_total // 2
    col_start = lax.axis_index((XLO, *Y, *Z, CORE)) * columns
    place = jnp.stack([lax.axis_index(HEAD), lax.axis_index(CORE), col_start]).astype(jnp.int32)
    weights = head_weights.T
    fetch = [pltpu.VMEM((depth, columns, width), bf16), pltpu.SemaphoreType.DMA((depth,))]

    mine = copies(copies(hidden, GATHER_FAR), GATHER_NEAR)
    other = lax.ppermute(mine, CORE, SWAP)
    shape = (xlo, zlo, yhi * ylo, zhi, rows, width)
    part = on_core(first_kernel, array((columns, row_total)), 1, "first", scratch=fetch, hbm=1)(
        place, mine.reshape(shape), weights
    )
    kept, sent = on_core(
        second_kernel, [array((columns, half))] * 2, 2, "second", scratch=fetch, hbm=1
    )(place, part, other.reshape(shape), weights)

    got = lax.ppermute(sent, HEAD, SWAP)
    narrow, wide = lax.axis_size(NARROW), lax.axis_size(WIDE)
    stats = on_core(stats_kernel, array((narrow, 8, half)), 2, "stats")(place, kept, got)
    kept_late, stats = lax.optimization_barrier((kept, stats))
    late = lax.ppermute(kept_late, HEAD, SWAP)
    stats = lax.all_to_all(stats, NARROW, 0, 0, tiled=True)
    stats = on_core(merge_kernel, array((wide, 8, half)), 1, "merge", False)(stats)
    stats = lax.all_to_all(stats, WIDE, 0, 0, tiled=True)
    final = on_core(final_kernel, array((8, row_total)), 1, "final", False)(stats)

    line = lambda a: a.reshape(1, row_total)
    padded = -(-columns // LANES) * LANES
    turned, sent_part = on_core(
        sent_kernel,
        [array((row_total, padded), bf16), array((depth, row_total, width), bf16)],
        8,
        "sent_part",
        scratch=[pltpu.VMEM((padded, row_total), f32), *fetch],
        hbm=1,
    )(
        place, kept, got, sent, late, final, line(token_ids), line(kl_weight), line(advantage),
        weights,
    )
    back = lax.ppermute(sent_part, CORE, SWAP)
    pair_sum = on_core(
        pair_kernel,
        array((ylo, zlo, xlo, yhi, zhi, rows, width), bf16),
        2,
        "pair_sum",
        scratch=fetch,
        hbm=1,
    )(place, turned, back, weights)
    near = exchange_sum(pair_sum.reshape(ylo * zlo, -1, width), REDUCE_NEAR).astype(bf16)
    hidden_grad = exchange_sum(near.reshape(-1, rows, width), REDUCE_FAR).T
    return (hidden_grad, final[2], final[1])


def solution(mesh):
    finer = Mesh(mesh.devices.reshape(2, 2, 4, 2, 4, 2, 2), (*WIDE, *NARROW))
    return jax.shard_map(
        body,
        mesh=finer,
        in_specs=(P(WIDE, NARROW), P(None, (*WIDE, *NARROW)), P(), P(), P()),
        out_specs=(P(NARROW, WIDE), P(), P()),
        check_vma=False,
    )
```

time: 158 us -> 151 us (0.956)
  waiting for transfers between devices: 44.8 us -> 25.4 us
  blocking collectives: 62.1 us -> 73 us
  Pallas kernels: 11.8 us -> 17.6 us
  local copies, waits for them, and re-layouts: 6.09 us -> 1.38 us
    all_to_all x1, waiting for transfers between devices: 29.5 us -> 11.9 us  [exchange_sum(): return jnp.sum(lax.all_to_all(parts, axes, 0, 0, tiled=True).astype(f32), 0)]
    all_to_all x1 -> x3, blocking collectives: 48.3 us -> 58.2 us  [the longest x2 42.2 us: copies(): lax.all_to_all(jnp.broadcast_to(block[None], (count, *block.shape)), axes...]
    pallas_call x5 -> x7, Pallas kernels: 11.8 us -> 17.6 us  [the longest x1 4.41 us: body(): on_core(pair_kernel, array((ylo, zlo, xlo, yhi, zhi, rows, width), bf16),...]
    unnamed x10 -> x6, local copies, waits for them, and re-layouts: 4.75 us -> 0.02 us
    all_to_all x1, starting transfers between devices: 6.19 us -> 3.87 us  [exchange_sum(): return jnp.sum(lax.all_to_all(parts, axes, 0, 0, tiled=True).astype(f32), 0)]
    ppermute x1, waiting for transfers between devices: 2.18 us -> 0.01 us  [body(): other = lax.ppermute(mine, CORE, SWAP)]
  transfers between devices with their start and end apart: 6 -> 6, of which waited for: 5 -> 4; matrix products, arithmetic and copies ran while one was open for 0% -> 0% of each run, Pallas kernels for 0% -> 3%
where the time goes in v2:
time: 151 us; the launch traced here: 149 us
  blocking collectives  73 us (48%)
  starting transfers between devices  28.6 us (19%)
  waiting for transfers between devices  25.4 us (17%)
  Pallas kernels  17.6 us (12%)
  other arithmetic  1.62 us (1%)
    all_to_all x2, blocking collectives, copies(): lax.all_to_all(jnp.broadcast_to(block[None], (count, *block.shape)), axes...  42.2 us
    all_to_all x1, blocking collectives, exchange_sum(): return jnp.sum(lax.all_to_all(parts, axes, 0, 0, tiled=True).astype(f32), 0)  16 us
    all_to_all x1, blocking collectives, body(): stats = lax.all_to_all(stats, WIDE, 0, 0, tiled=True)  14.8 us
    all_to_all x1, waiting for transfers between devices, exchange_sum(): return jnp.sum(lax.all_to_all(parts, axes, 0, 0, tiled=True).astype(f32), 0)  11.9 us
    ppermute x1, waiting for transfers between devices, body(): got = lax.ppermute(sent, HEAD, SWAP)  7.83 us
    ppermute x1, starting transfers between devices, body(): other = lax.ppermute(mine, CORE, SWAP)  6.25 us
    all_to_all x1, starting transfers between devices, body(): stats = lax.all_to_all(stats, NARROW, 0, 0, tiled=True)  5.72 us
    pallas_call x1, Pallas kernels, body(): on_core(pair_kernel, array((ylo, zlo, xlo, yhi, zhi, rows, width), bf16),...  4.41 us
  transfers between devices with their start and end apart: 6, of which 4 were waited for; matrix products, arithmetic and copies ran while one was open for 0% of the time, Pallas kernels for 3%

profile of v2, /device:TPU:1, one launch (start us, length us, event | category | flops | bytes accessed | tf_op | source)
XLA Modules:
  0.0 148.5 jit_solution(12503561412910691353)
XLA Ops:
  0.6 0.7 broadcast_in_dim.4
  1.3 28.4 %all_to_all.30 = bf16[32,16,256]{2,1,0:T(8,128)(2,1)S(1)} all-to-all(bf16[32,16,256]{2,1,0:T(8,128)(2,1)S(1)} %broadcast_in_dim.4), channel_id=1, replica_groups=mesh['head'=2,'xlo'=2,'yhi'=4,'ylo'=2,'zhi'=4,'zlo'=2,'core'=2] {'yhi','..., dimensions={0} | all-to-all | bytes 524288 | tf_op jit(solution)/shard_map/all_to_all | solution.py:219
  29.8 0.1 broadcast_in_dim.5
  29.8 13.8 %all_to_all.31 = bf16[4,32,16,256]{3,2,1,0:T(8,128)(2,1)S(1)} all-to-all(bf16[4,32,16,256]{3,2,1,0:T(8,128)(2,1)S(1)} %broadcast_in_dim.5), channel_id=1, replica_groups=mesh['head'=2,'xlo'=2,'yhi'=4,'ylo'=2,'zhi'=4,'zlo'=2,'core'=2] {'xlo','..., dimensions={0} | all-to-all | bytes 2097152 | tf_op jit(solution)/shard_map/all_to_all | solution.py:219
  43.7 6.3 %collective-permute-start = (bf16[4,32,16,256]{3,2,1,0:T(8,128)(2,1)S(1)}, bf16[4,32,16,256]{3,2,1,0:T(8,128)(2,1)S(1)}, u32[]{:S(2)}, u32[]{:S(2)}) collective-permute-start(bf16[4,32,16,256]{3,2,1,0:T(8,128)(2,1)S(1)} %all_to_all.31), channel_id=1, source_target_pairs={{0,1},{1,0},{2,3},{3,2},{4,5},{5,4},{6,7},{7,6},{8,9},{9,8},{10,11... | collective-permute-start | bytes 3145736 | tf_op jit(solution)/shard_map/ppermute | solution.py:241
  50.0 0.1 pad_add_fusion.place
  50.0 3.6 %first.1.part = f32[592,256]{1,0:T(8,128)S(1)} custom-call(s32[3]{0:T(128)S(1)} %pad_add_fusion.place, bf16[2,2,8,4,16,256]{5,4,3,2,1,0:T(8,128)(2,1)S(1)} %bitcast.14, bf16[592,4096]{1,0:T(8,128)(2,1)} %bitcast.20), custom_call_target="tpu_custom_call" | custom-call | tf_op jit(solution)/shard_map/first/pallas_call | solution.py:243
  53.7 0.0 copy-start
  53.7 0.0 copy-start.1
  53.7 0.0 copy-start.2
  53.7 0.0 collective-permute-done
  53.7 3.7 %second.1 = (f32[592,128]{1,0:T(8,128)S(1)}, f32[592,128]{1,0:T(8,128)S(1)}) custom-call(s32[3]{0:T(128)S(1)} %pad_add_fusion.place, f32[592,256]{1,0:T(8,128)S(1)} %first.1.part, bf16[2,2,8,4,16,256]{5,4,3,2,1,0:T(8,128)(2,1)S(1)} %bitcast.16, bf16[592,4096]{1,0:T(8,128)(2,1)} %bitcast.21), custom_call_target="tpu_custom_call" | custom-call | tf_op jit(solution)/shard_map/second/pallas_call | solution.py:246
  57.4 4.4 %collective-permute-start.1 = (f32[592,128]{1,0:T(8,128)S(1)}, f32[592,128]{1,0:T(8,128)S(1)}, u32[]{:S(2)}, u32[]{:S(2)}) collective-permute-start(f32[592,128]{1,0:T(8,128)S(1)} %get-tuple-element.10.sent), channel_id=1, source_target_pairs={{0,256},{256,0},{1,257},{257,1},{2,258},{258,2},{3,259},{259,3},{4... | collective-permute-start | bytes 909320 | tf_op jit(solution)/shard_map/ppermute | solution.py:250
  61.7 7.8 %collective-permute-done.1.got = f32[592,128]{1,0:T(8,128)S(1)} collective-permute-done((f32[592,128]{1,0:T(8,128)S(1)}, f32[592,128]{1,0:T(8,128)S(1)}, u32[]{:S(2)}, u32[]{:S(2)}) %collective-permute-start.1) | collective-permute-done | bytes 303136 | tf_op jit(solution)/shard_map/ppermute | solution.py:250
  69.6 1.4 stats.1
  71.0 5.7 %all-to-all-start.2 = ((f32[16,8,128]{2,1,0:T(8,128)}), f32[16,8,128]{2,1,0:T(8,128)S(1)}, u32[]{:S(2)}, u32[]{:S(2)}) async-start(f32[16,8,128]{2,1,0:T(8,128)} %stats.1), calls=%async_computation.2 | async-start | bytes 131072 | tf_op jit(solution)/shard_map/all_to_all | solution.py:255
  76.7 4.4 %collective-permute-start.2 = (f32[592,128]{1,0:T(8,128)S(1)}, f32[592,128]{1,0:T(8,128)S(1)}, u32[]{:S(2)}, u32[]{:S(2)}) collective-permute-start(f32[592,128]{1,0:T(8,128)S(1)} %get-tuple-element.11.kept), channel_id=1, source_target_pairs={{0,256},{256,0},{1,257},{257,1},{2,258},{258,2},{3,259},{259,3},{4... | collective-permute-start | bytes 909320 | tf_op jit(solution)/shard_map/ppermute | solution.py:254
  81.1 3.4 %all-to-all-done.2.tiles = f32[16,8,128]{2,1,0:T(8,128)S(1)} async-done(((f32[16,8,128]{2,1,0:T(8,128)}), f32[16,8,128]{2,1,0:T(8,128)S(1)}, u32[]{:S(2)}, u32[]{:S(2)}) %all-to-all-start.2) | async-done | bytes 65568 | tf_op jit(solution)/shard_map/all_to_all | solution.py:255
  84.6 14.8 %all_to_all.32.tiles = f32[32,8,128]{2,1,0:T(8,128)S(1)} all-to-all(f32[32,8,128]{2,1,0:T(8,128)S(1)} %merge.1), channel_id=1, replica_groups=mesh['head'=2,'xlo'=2,'yhi'=4,'ylo'=2,'zhi'=4,'zlo'=2,'core'=2] {'head',..., dimensions={0} | all-to-all | bytes 262144 | tf_op jit(solution)/shard_map/all_to_all | solution.py:257
  99.4 0.1 final.1
  99.5 0.0 collective-permute-done.2.late
  99.5 0.0 copy-done
  99.5 0.0 copy-done.1
  99.5 0.0 copy-done.2
  99.5 4.4 %sent_part.1 = (bf16[256,640]{1,0:T(8,128)(2,1)S(1)}, bf16[8,256,256]{2,1,0:T(8,128)(2,1)S(1)}) custom-call(s32[3]{0:T(128)S(1)} %pad_add_fusion.place, f32[592,128]{1,0:T(8,128)S(1)} %get-tuple-element.11.kept, f32[592,128]{1,0:T(8,128)S(1)} %collective-permute-done.1.got, f32[592,128]{1,0:T(8,128)S(1)} %get-tuple-element.10.sent, ...), custom_call_target="tpu_custom_call" | custom-call | tf_op jit(solution)/shard_map/sent_part/pallas_call | solution.py:262
  103.9 4.0 %collective-permute-start.3 = (bf16[8,256,256]{2,1,0:T(8,128)(2,1)S(1)}, bf16[8,256,256]{2,1,0:T(8,128)(2,1)S(1)}, u32[]{:S(2)}, u32[]{:S(2)}) collective-permute-start(bf16[8,256,256]{2,1,0:T(8,128)(2,1)S(1)} %get-tuple-element.14), channel_id=1, source_target_pairs={{0,1},{1,0},{2,3},{3,2},{4,5},{5,4},{6,7},{7,6},{8,9},{9,8},{10,11... | collective-permute-start | bytes 3145736 | tf_op jit(solution)/shard_map/ppermute | solution.py:273
  108.0 2.3 %collective-permute-done.3.back = bf16[8,256,256]{2,1,0:T(8,128)(2,1)S(1)} collective-permute-done((bf16[8,256,256]{2,1,0:T(8,128)(2,1)S(1)}, bf16[8,256,256]{2,1,0:T(8,128)(2,1)S(1)}, u32[]{:S(2)}, u32[]{:S(2)}) %collective-permute-start.3) | collective-permute-done | bytes 1048608 | tf_op jit(solution)/shard_map/ppermute | solution.py:273
  110.2 4.4 %pair_sum.1 = bf16[2,2,2,4,4,16,256]{6,5,4,3,2,1,0:T(8,128)(2,1)S(1)} custom-call(s32[3]{0:T(128)S(1)} %pad_add_fusion.place, bf16[256,640]{1,0:T(8,128)(2,1)S(1)} %get-tuple-element.13.turned, bf16[8,256,256]{2,1,0:T(8,128)(2,1)S(1)} %collective-permute-done.3.back, bf16[592,4096]{1,0:T(8,128)(2,1)} %bitcast.23), custom_call_target="tpu_custom_call" | custom-call | tf_op jit(solution)/shard_map/pair_sum/pallas_call | solution.py:274
  114.6 16.0 %all_to_all.33 = bf16[4,512,256]{2,1,0:T(8,128)(2,1)S(1)} all-to-all(bf16[4,512,256]{2,1,0:T(8,128)(2,1)S(1)} %bitcast.15), channel_id=1, replica_groups=mesh['head'=2,'xlo'=2,'yhi'=4,'ylo'=2,'zhi'=4,'zlo'=2,'core'=2] {'ylo','..., dimensions={0} | all-to-all | bytes 2097152 | tf_op jit(solution)/shard_map/all_to_all | solution.py:225
  130.6 0.9 reduce_sum.21
  131.5 3.9 %all-to-all-start.5 = ((bf16[32,16,256]{2,1,0:T(8,128)(2,1)}), bf16[32,16,256]{2,1,0:T(8,128)(2,1)S(1)}, u32[]{:S(2)}, u32[]{:S(2)}) async-start(bf16[32,16,256]{2,1,0:T(8,128)(2,1)} %bitcast.10), calls=%async_computation.5 | async-start | bytes 524288 | tf_op jit(solution)/shard_map/all_to_all | solution.py:225
  135.4 0.6 fusion
  136.0 11.9 %all-to-all-done.5 = bf16[32,16,256]{2,1,0:T(8,128)(2,1)S(1)} async-done(((bf16[32,16,256]{2,1,0:T(8,128)(2,1)}), bf16[32,16,256]{2,1,0:T(8,128)(2,1)S(1)}, u32[]{:S(2)}, u32[]{:S(2)}) %all-to-all-start.5) | async-done | bytes 262176 | tf_op jit(solution)/shard_map/all_to_all | solution.py:225
  147.9 0.7 convert_reduce_fusion
  (1 shorter events, 0.0 us)
Async XLA Ops:
  43.7 10.0 %collective-permute-start = (bf16[4,32,16,256]{3,2,1,0:T(8,128)(2,1)S(1)}, bf16[4,32,16,256]{3,2,1,0:T(8,128)(2,1)S(1)}, u32[]{:S(2)}, u32[]{:S(2)}) collective-permute-start(bf16[4,32,16,256]{3,2,1,0:T(8,128)(2,1)S(1)} %all_to_all.31), channel_id=1, source_target_pairs={{0,1},{1,0},{2,3},{3,2},{4,5},{5,4},{6,7},{7,6},{8,9},{9,8},{10,11... | collective-permute-start | bytes 3145736 | tf_op jit(solution)/shard_map/ppermute | solution.py:241
  53.7 45.8 %copy-start = (s32[256]{0:T(256)S(1)}, s32[256]{0:T(256)}, u32[]{:S(2)}) copy-start(s32[256]{0:T(256)} %param.7) | copy-start | bytes 3076
  53.7 45.8 %copy-start.1 = (f32[256]{0:T(256)S(1)}, f32[256]{0:T(256)}, u32[]{:S(2)}) copy-start(f32[256]{0:T(256)} %param.8) | copy-start | bytes 3076
  53.7 45.8 %copy-start.2 = (f32[256]{0:T(256)S(1)}, f32[256]{0:T(256)}, u32[]{:S(2)}) copy-start(f32[256]{0:T(256)} %param.9) | copy-start | bytes 3076
  57.4 12.2 %collective-permute-start.1 = (f32[592,128]{1,0:T(8,128)S(1)}, f32[592,128]{1,0:T(8,128)S(1)}, u32[]{:S(2)}, u32[]{:S(2)}) collective-permute-start(f32[592,128]{1,0:T(8,128)S(1)} %get-tuple-element.10.sent), channel_id=1, source_target_pairs={{0,256},{256,0},{1,257},{257,1},{2,258},{258,2},{3,259},{259,3},{4... | collective-permute-start | bytes 909320 | tf_op jit(solution)/shard_map/ppermute | solution.py:250
  71.0 13.5 %all-to-all-start.2 = ((f32[16,8,128]{2,1,0:T(8,128)}), f32[16,8,128]{2,1,0:T(8,128)S(1)}, u32[]{:S(2)}, u32[]{:S(2)}) async-start(f32[16,8,128]{2,1,0:T(8,128)} %stats.1), calls=%async_computation.2 | async-start | bytes 131072 | tf_op jit(solution)/shard_map/all_to_all | solution.py:255
  76.7 22.8 %collective-permute-start.2 = (f32[592,128]{1,0:T(8,128)S(1)}, f32[592,128]{1,0:T(8,128)S(1)}, u32[]{:S(2)}, u32[]{:S(2)}) collective-permute-start(f32[592,128]{1,0:T(8,128)S(1)} %get-tuple-element.11.kept), channel_id=1, source_target_pairs={{0,256},{256,0},{1,257},{257,1},{2,258},{258,2},{3,259},{259,3},{4... | collective-permute-start | bytes 909320 | tf_op jit(solution)/shard_map/ppermute | solution.py:254
  103.9 6.3 %collective-permute-start.3 = (bf16[8,256,256]{2,1,0:T(8,128)(2,1)S(1)}, bf16[8,256,256]{2,1,0:T(8,128)(2,1)S(1)}, u32[]{:S(2)}, u32[]{:S(2)}) collective-permute-start(bf16[8,256,256]{2,1,0:T(8,128)(2,1)S(1)} %get-tuple-element.14), channel_id=1, source_target_pairs={{0,1},{1,0},{2,3},{3,2},{4,5},{5,4},{6,7},{7,6},{8,9},{9,8},{10,11... | collective-permute-start | bytes 3145736 | tf_op jit(solution)/shard_map/ppermute | solution.py:273
  131.5 16.3 %all-to-all-start.5 = ((bf16[32,16,256]{2,1,0:T(8,128)(2,1)}), bf16[32,16,256]{2,1,0:T(8,128)(2,1)S(1)}, u32[]{:S(2)}, u32[]{:S(2)}) async-start(bf16[32,16,256]{2,1,0:T(8,128)(2,1)} %bitcast.10), calls=%async_computation.5 | async-start | bytes 524288 | tf_op jit(solution)/shard_map/all_to_all | solution.py:225

commit v3 on v2

--- a/solution.py
+++ b/solution.py
@@ -12,7 +12,8 @@
 NARROW = (*Z, CORE)
 WIDE = (HEAD, XLO, *Y)
 GATHER_FAR, GATHER_NEAR = (*Y, ZHI), (XLO, ZLO)
-REDUCE_NEAR, REDUCE_FAR = (YLO, ZLO), (XLO, YHI, ZHI)
+STATS_NEAR, STATS_FAR = (HEAD, XLO, YLO, ZLO, CORE), (YHI, ZHI)
+REDUCE_NEAR, REDUCE_FAR = (XLO, YLO, ZLO), (YHI, ZHI)
 
 BETA = 0.2
 SWAP = [(0, 1), (1, 0)]
@@ -20,48 +21,78 @@
 STEP = 16
 f32 = jnp.float32
 bf16 = jnp.bfloat16
+ANY = pl.BlockSpec(memory_space=pl.ANY)
 VMEM = pl.BlockSpec(memory_space=pltpu.VMEM)
-HBM = pl.BlockSpec(memory_space=pltpu.HBM)
 SMEM = pl.BlockSpec(memory_space=pltpu.SMEM)
-WIDE_PARAMS = pltpu.CompilerParams(vmem_limit_bytes=50 << 20)
+WIDE_PARAMS = pltpu.CompilerParams(vmem_limit_bytes=48 << 20)
+WIDER_PARAMS = pltpu.CompilerParams(vmem_limit_bytes=50 << 20)
 PARAMS = pltpu.CompilerParams(vmem_limit_bytes=16 << 20)
 
 
-def fetches(weights, core, buffer, sems):
-    depth, _, width = buffer.shape
+def hold_kernel(place, weights, mine, other, sems):
+    depth = sems.shape[1]
+    width = mine.shape[1] // depth
     copies = []
-    for z in range(depth):
-        start = pl.multiple_of((2 * z + core) * width, width)
-        copies.append(
-            pltpu.make_async_copy(weights.at[:, pl.ds(start, width)], buffer.at[z], sems.at[z])
-        )
-        copies[z].start()
+    for side, out in enumerate((mine, other)):
+        core = place[1] if side == 0 else 1 - place[1]
+        for z in range(depth):
+            start = pl.multiple_of((2 * z + core) * width, width)
+            source = weights.at[:, pl.ds(start, width)]
+            target = out.at[:, z * width : (z + 1) * width]
+            copies.append(pltpu.make_async_copy(source, target, sems.at[side, z]))
+            copies[-1].start()
+    for copy in copies:
+        copy.wait()
+
+
+def held(place, weights, depth):
+    columns, features = weights.shape
+    half = pltpu.HBM((columns, features // 2), weights.dtype)
+    return pl.pallas_call(
+        hold_kernel,
+        in_specs=[SMEM, ANY],
+        out_specs=[ANY, ANY],
+        out_shape=[half, half],
+        scratch_shapes=[pltpu.SemaphoreType.DMA((2, depth))],
+        compiler_params=PARAMS,
+        name="hold",
+    )(place, weights)
+
+
+def fetch(sources, targets, sems):
+    copies = [
+        pltpu.make_async_copy(source, target, sems.at[k])
+        for k, (source, target) in enumerate(zip(sources, targets))
+    ]
+    for copy in copies:
+        copy.start()
     return copies
 
 
-def products(blocks, copies, buffer):
+def flatten(blocks, flat):
     xlo, zlo, y, zhi, rows, width = blocks.shape
-    total = None
-    for z, copy in enumerate(copies):
-        hi, lo = z // zlo, z % zlo
-        copy.wait()
-        part = lax.dot_general(
-            buffer[z],
-            blocks[:, lo, :, hi].reshape(xlo * y * rows, width),
-            (((1,), (1,)), ((), ())),
-            preferred_element_type=f32,
-        )
-        total = part if total is None else total + part
-    return total
-
-
-def first_kernel(place, mine, weights, out, buffer, sems):
-    out[...] = products(mine, fetches(weights, place[1], buffer, sems), buffer)
-
-
-def second_kernel(place, part, other, weights, kept, sent, buffer, sems):
-    copies = fetches(weights, 1 - place[1], buffer, sems)
-    total = part[...] + products(other, copies, buffer)
+    for z in range(zhi * zlo):
+        part = blocks[:, z % zlo, :, z // zlo].reshape(xlo * y * rows, width)
+        flat[:, z * width : (z + 1) * width] = part
+
+
+def product(weights, flat):
+    return lax.dot_general(
+        weights[...], flat[...], (((1,), (1,)), ((), ())), preferred_element_type=f32
+    )
+
+
+def first_kernel(mine, w_mine, w_other, out, next_weights, flat, here, sems):
+    copies = fetch((w_mine, w_other), (here, next_weights), sems)
+    flatten(mine, flat)
+    copies[0].wait()
+    out[...] = product(here, flat)
+    copies[1].wait()
+
+
+def second_kernel(place, part, other, weights, kept, sent, flat):
+    flatten(other, flat)
+    total = part[...] + product(weights, flat)
     half = kept.shape[1]
 
     @pl.when(place[0] == 0)
@@ -112,25 +143,26 @@
     return lse[0:1], cross, lse[2:3]
 
 
+def both_heads(tiles):
+    sides = [merged(tiles[k]) for k in range(2)]
+    return [jnp.concatenate(pair, 1) for pair in zip(*sides)]
+
+
 def merge_kernel(tiles, out):
-    out[...] = spread(merged(tiles[...]), out.shape)
+    out[...] = spread(both_heads(tiles), out.shape)
 
 
 def final_kernel(tiles, out):
-    count = tiles.shape[0] // 2
-    half = tiles.shape[2]
-    for k in range(2):
-        policy_lse, cross, mixture_lse = merged(tiles[k * count : (k + 1) * count])
-        divergence = cross - policy_lse + mixture_lse
-        lines = (policy_lse, divergence, mixture_lse)
-        out[:, k * half : (k + 1) * half] = spread(lines, (1, 8, half))[0]
+    policy_lse, cross, mixture_lse = merged(tiles[...])
+    lines = (policy_lse, cross - policy_lse + mixture_lse, mixture_lse)
+    out[...] = spread(lines, (1, *out.shape))[0]
 
 
 def sent_kernel(
-    place, kept, got, sent, late, final, ids, kl_weight, advantage, weights,
-    turned, sent_out, flat, buffer, sems,
+    place, kept, got, sent, late, final, ids, kl_weight, advantage, w_other,
+    turned, sent_out, flat, here, sems,
 ):
-    copies = fetches(weights, 1 - place[1], buffer, sems)
+    copies = fetch((w_other,), (here,), sems)
     columns, half = kept.shape
     padded = flat.shape[0]
 
@@ -175,37 +207,46 @@
     def _():
         fill((sent, late), (kept, got), False)
 
-    for z, part in sums(turned, copies, buffer):
-        sent_out[z] = part.astype(bf16)
-
-
-def sums(turned, copies, buffer):
-    grad = turned[:, : buffer.shape[1]]
-    for z, copy in enumerate(copies):
-        copy.wait()
-        yield z, lax.dot_general(
-            grad, buffer[z], (((1,), (0,)), ((), ())), preferred_element_type=f32
+    copies[0].wait()
+    for at, part in sums(turned, here):
+        sent_out[:, at] = part.astype(bf16)
+
+
+def sums(turned, weights, step=512):
+    columns, features = weights.shape
+    grad = turned[:, :columns]
+    for start in range(0, features, step):
+        at = slice(start, start + step)
+        yield at, lax.dot_general(
+            grad, weights[:, at], (((1,), (0,)), ((), ())), preferred_element_type=f32
         )
 
 
-def pair_kernel(place, turned, back, weights, out, buffer, sems):
-    ylo, zlo, xlo, yhi, zhi, rows, width = out.shape
-    copies = fetches(weights, place[1], buffer, sems)
-    for z, part in sums(turned, copies, buffer):
-        whole = (part + back[z].astype(f32)).astype(bf16)
+def own_kernel(turned, w_mine, out, here, sems):
+    copies = fetch((w_mine,), (here,), sems)
+    copies[0].wait()
+    for at, part in sums(turned, here):
+        out[:, at] = part
+
+
+def pair_kernel(partial, back, out):
+    xlo, ylo, zlo, yhi, zhi, rows, width = out.shape
+    for z in range(zhi * zlo):
+        at = slice(z * width, (z + 1) * width)
+        whole = (partial[:, at] + back[:, at].astype(f32)).astype(bf16)
         whole = whole.reshape(xlo, yhi, ylo, rows, width)
         for lo in range(ylo):
-            out[lo, z % zlo, :, :, z // zlo] = whole[:, :, lo]
+            out[:, lo, z % zlo, :, z // zlo] = whole[:, :, lo]
 
 
 def on_core(kernel, out_shape, count, name, scalars=True, scratch=(), hbm=0):
     return pl.pallas_call(
         kernel,
-        in_specs=[SMEM] * scalars + [VMEM] * count + [HBM] * hbm,
+        in_specs=[SMEM] * scalars + [VMEM] * count + [ANY] * hbm,
         out_specs=jax.tree.map(lambda _: VMEM, out_shape),
         out_shape=out_shape,
         scratch_shapes=scratch,
-        compiler_params=WIDE_PARAMS if hbm else PARAMS,
+        compiler_params=(PARAMS, WIDER_PARAMS, WIDE_PARAMS)[hbm],
         name=name,
     )
 
@@ -234,52 +275,61 @@
     half = row_total // 2
     col_start = lax.axis_index((XLO, *Y, *Z, CORE)) * columns
     place = jnp.stack([lax.axis_index(HEAD), lax.axis_index(CORE), col_start]).astype(jnp.int32)
-    weights = head_weights.T
-    fetch = [pltpu.VMEM((depth, columns, width), bf16), pltpu.SemaphoreType.DMA((depth,))]
-
-    mine = copies(copies(hidden, GATHER_FAR), GATHER_NEAR)
+    w_mine, w_other = held(place, head_weights.T, depth)
+    flat = [pltpu.VMEM((row_total, depth * width), bf16)]
+
+    far = copies(hidden, GATHER_FAR)
+    far, w_mine, w_other = lax.optimization_barrier((far, w_mine, w_other))
+    mine = copies(far, GATHER_NEAR)
     other = lax.ppermute(mine, CORE, SWAP)
     shape = (xlo, zlo, yhi * ylo, zhi, rows, width)
-    part = on_core(first_kernel, array((columns, row_total)), 1, "first", scratch=fetch, hbm=1)(
-        place, mine.reshape(shape), weights
-    )
+    w_half = array((columns, depth * width), bf16)
+    buffers = [pltpu.VMEM(w_half.shape, bf16), pltpu.SemaphoreType.DMA((2,))]
+    part, w_next = on_core(
+        first_kernel,
+        [array((columns, row_total)), w_half],
+        1,
+        "first",
+        False,
+        scratch=flat + buffers,
+        hbm=2,
+    )(mine.reshape(shape), w_mine, w_other)
     kept, sent = on_core(
-        second_kernel, [array((columns, half))] * 2, 2, "second", scratch=fetch, hbm=1
-    )(place, part, other.reshape(shape), weights)
+        second_kernel, [array((columns, half))] * 2, 3, "second", scratch=flat
+    )(place, part, other.reshape(shape), w_next)
 
     got = lax.ppermute(sent, HEAD, SWAP)
-    narrow, wide = lax.axis_size(NARROW), lax.axis_size(WIDE)
-    stats = on_core(stats_kernel, array((narrow, 8, half)), 2, "stats")(place, kept, got)
+    near, far = lax.axis_size(STATS_NEAR), lax.axis_size(STATS_FAR)
+    stats = on_core(stats_kernel, array((near, 8, half)), 2, "stats")(place, kept, got)
     kept_late, stats = lax.optimization_barrier((kept, stats))
     late = lax.ppermute(kept_late, HEAD, SWAP)
-    stats = lax.all_to_all(stats, NARROW, 0, 0, tiled=True)
-    stats = on_core(merge_kernel, array((wide, 8, half)), 1, "merge", False)(stats)
-    stats = lax.all_to_all(stats, WIDE, 0, 0, tiled=True)
+    stats = lax.all_to_all(stats, STATS_NEAR, 0, 0, tiled=True).reshape(2, near // 2, 8, half)
+    stats = on_core(merge_kernel, array((far, 8, row_total)), 1, "merge", False)(stats)
+    stats = lax.all_to_all(stats, STATS_FAR, 0, 0, tiled=True)
     final = on_core(final_kernel, array((8, row_total)), 1, "final", False)(stats)
 
     line = lambda a: a.reshape(1, row_total)
     padded = -(-columns // LANES) * LANES
+    wide_rows = (row_total, depth * width)
     turned, sent_part = on_core(
         sent_kernel,
-        [array((row_total, padded), bf16), array((depth, row_total, width), bf16)],
+        [array((row_total, padded), bf16), array(wide_rows, bf16)],
         8,
         "sent_part",
-        scratch=[pltpu.VMEM((padded, row_total), f32), *fetch],
+        scratch=[pltpu.VMEM((padded, row_total), f32), *buffers],
         hbm=1,
     )(
         place, kept, got, sent, late, final, line(token_ids), line(kl_weight), line(advantage),
-        weights,
+        w_other,
     )
     back = lax.ppermute(sent_part, CORE, SWAP)
+    partial = on_core(own_kernel, array(wide_rows), 1, "own", False, scratch=buffers, hbm=1)(
+        turned, w_mine
+    )
     pair_sum = on_core(
-        pair_kernel,
-        array((ylo, zlo, xlo, yhi, zhi, rows, width), bf16),
-        2,
-        "pair_sum",
-        scratch=fetch,
-        hbm=1,
-    )(place, turned, back, weights)
-    near = exchange_sum(pair_sum.reshape(ylo * zlo, -1, width), REDUCE_NEAR).astype(bf16)
+        pair_kernel, array((xlo, ylo, zlo, yhi, zhi, rows, width), bf16), 2, "pair_sum", False
+    )(partial, back)
+    near = exchange_sum(pair_sum.reshape(xlo * ylo * zlo, -1, width), REDUCE_NEAR).astype(bf16)
     hidden_grad = exchange_sum(near.reshape(-1, rows, width), REDUCE_FAR).T
     return (hidden_grad, final[2], final[1])
 

time: 151 us -> 143 us (0.947); the launches traced: 149 us -> 143 us
  blocking collectives: 73 us -> 46.9 us
  starting transfers between devices: 28.6 us -> 46.8 us
  Pallas kernels: 17.6 us -> 14.5 us
  local copies, waits for them, and re-layouts: 1.38 us -> 4.47 us
  waiting for transfers between devices: 25.4 us -> 27.8 us
    all_to_all x2 -> x1, blocking collectives: 42.2 us -> 13.8 us  [copies(): lax.all_to_all(jnp.broadcast_to(block[None], (count, *block.shape)), axes...]
    all_to_all x1 -> x2, starting transfers between devices: 5.72 us -> 24 us  [the longest x1 16.5 us: copies(): lax.all_to_all(jnp.broadcast_to(block[None], (count, *block.shape)), axes...]
    all_to_all x1 -> x2, waiting for transfers between devices: 3.4 us -> 9.14 us  [the longest x1 6.75 us: copies(): lax.all_to_all(jnp.broadcast_to(block[None], (count, *block.shape)), axes...]
    pallas_call x6 -> x8, Pallas kernels: 17.6 us -> 14.4 us  [the longest x1 3.23 us: body(): on_core(sent_kernel, [array((row_total, padded), bf16), array(wide_rows,...]
    unnamed x6 -> x8, local copies, waits for them, and re-layouts: 0.02 us -> 2.39 us
    ppermute x1, waiting for transfers between devices: 2.26 us -> 0.01 us  [body(): back = lax.ppermute(sent_part, CORE, SWAP)]
    all_to_all x1, blocking collectives: 16 us -> 17.7 us  [exchange_sum(): return jnp.sum(lax.all_to_all(parts, axes, 0, 0, tiled=True).astype(f32), 0)]
  transfers between devices with their start and end apart: 6 -> 7, of which waited for: 4 -> 4; matrix products, arithmetic and copies ran while one was open for 0% -> 0% of each run, Pallas kernels for 3% -> 6%
where the time goes in v3:
time: 143 us
  blocking collectives  46.9 us (33%)
  starting transfers between devices  46.8 us (33%)
  waiting for transfers between devices  27.8 us (19%)
  Pallas kernels  14.5 us (10%)
  local copies, waits for them, and re-layouts  4.47 us (3%)
  other arithmetic  1.51 us (1%)
    all_to_all x1, blocking collectives, exchange_sum(): return jnp.sum(lax.all_to_all(parts, axes, 0, 0, tiled=True).astype(f32), 0)  17.7 us
    all_to_all x1, starting transfers between devices, copies(): lax.all_to_all(jnp.broadcast_to(block[None], (count, *block.shape)), axes...  16.5 us
    all_to_all x1, blocking collectives, body(): stats = lax.all_to_all(stats, STATS_FAR, 0, 0, tiled=True)  15.4 us
    all_to_all x1, blocking collectives, copies(): lax.all_to_all(jnp.broadcast_to(block[None], (count, *block.shape)), axes...  13.8 us
    all_to_all x1, waiting for transfers between devices, exchange_sum(): return jnp.sum(lax.all_to_all(parts, axes, 0, 0, tiled=True).astype(f32), 0)  10.9 us
    ppermute x1, waiting for transfers between devices, body(): got = lax.ppermute(sent, HEAD, SWAP)  7.77 us
    all_to_all x1, starting transfers between devices, body(): lax.all_to_all(stats, STATS_NEAR, 0, 0, tiled=True)  7.55 us
    all_to_all x1, waiting for transfers between devices, copies(): lax.all_to_all(jnp.broadcast_to(block[None], (count, *block.shape)), axes...  6.75 us
  transfers between devices with their start and end apart: 7, of which 4 were waited for; matrix products, arithmetic and copies ran while one was open for 0% of the time, Pallas kernels for 6%

profile of v3, /device:TPU:1, one launch (start us, length us, event | category | flops | bytes accessed | tf_op | source)
XLA Modules:
  0.0 142.8 jit_solution(7511206600047094723)
XLA Ops:
  0.6 1.4 broadcast_in_dim.4
  2.1 16.5 %all-to-all-start = ((bf16[32,16,256]{2,1,0:T(8,128)(2,1)}), bf16[32,16,256]{2,1,0:T(8,128)(2,1)S(1)}, u32[]{:S(2)}, u32[]{:S(2)}) async-start(bf16[32,16,256]{2,1,0:T(8,128)(2,1)} %broadcast_in_dim.4), calls=%async_computation | async-start | bytes 524288 | tf_op jit(solution)/shard_map/all_to_all | solution.py:260
  18.6 0.1 pad_add_fusion.place
  18.7 0.0 copy-start
  18.7 2.4 %copy-done = bf16[4096,592]{0,1:T(8,128)(2,1)S(1)} copy-done((bf16[4096,592]{0,1:T(8,128)(2,1)S(1)}, bf16[4096,592]{0,1:T(8,128)(2,1)}, u32[]{:S(2)}) %copy-start) | copy-done | bytes 4849688
  21.0 2.9 %hold.1 = (bf16[592,2048]{1,0:T(8,128)(2,1)}, bf16[592,2048]{1,0:T(8,128)(2,1)}) custom-call(s32[3]{0:T(128)S(1)} %pad_add_fusion.place, bf16[592,4096]{1,0:T(8,128)(2,1)S(1)} %bitcast.15), custom_call_target="tpu_custom_call" | custom-call | tf_op jit(solution)/shard_map/hold/pallas_call | solution.py:51
  23.9 6.8 %all-to-all-done = bf16[32,16,256]{2,1,0:T(8,128)(2,1)S(1)} async-done(((bf16[32,16,256]{2,1,0:T(8,128)(2,1)}), bf16[32,16,256]{2,1,0:T(8,128)(2,1)S(1)}, u32[]{:S(2)}, u32[]{:S(2)}) %all-to-all-start) | async-done | bytes 262176 | tf_op jit(solution)/shard_map/all_to_all | solution.py:260
  30.7 0.1 broadcast_in_dim.5
  30.7 13.8 %all_to_all.30 = bf16[4,32,16,256]{3,2,1,0:T(8,128)(2,1)S(1)} all-to-all(bf16[4,32,16,256]{3,2,1,0:T(8,128)(2,1)S(1)} %broadcast_in_dim.5), channel_id=1, replica_groups=mesh['head'=2,'xlo'=2,'yhi'=4,'ylo'=2,'zhi'=4,'zlo'=2,'core'=2] {'xlo','..., dimensions={0} | all-to-all | bytes 2097152 | tf_op jit(solution)/shard_map/all_to_all | solution.py:260
  44.6 6.3 %collective-permute-start = (bf16[4,32,16,256]{3,2,1,0:T(8,128)(2,1)S(1)}, bf16[4,32,16,256]{3,2,1,0:T(8,128)(2,1)S(1)}, u32[]{:S(2)}, u32[]{:S(2)}) collective-permute-start(bf16[4,32,16,256]{3,2,1,0:T(8,128)(2,1)S(1)} %all_to_all.30), channel_id=1, source_target_pairs={{0,1},{1,0},{2,3},{3,2},{4,5},{5,4},{6,7},{7,6},{8,9},{9,8},{10,11... | collective-permute-start | bytes 3145736 | tf_op jit(solution)/shard_map/ppermute | solution.py:284
  50.8 2.5 %first.1 = (f32[592,256]{1,0:T(8,128)S(1)}, bf16[592,2048]{1,0:T(8,128)(2,1)S(1)}) custom-call(bf16[2,2,8,4,16,256]{5,4,3,2,1,0:T(8,128)(2,1)S(1)} %bitcast.16, bf16[592,2048]{1,0:T(8,128)(2,1)} %get-tuple-element.19.w_mine, bf16[592,2048]{1,0:T(8,128)(2,1)} %get-tuple-element.20.w_other), custom_call_target="tpu_custom_call" | custom-call | tf_op jit(solution)/shard_map/first/pallas_call | solution.py:288
  53.4 0.0 collective-permute-done
  53.4 0.0 copy-start.1
  53.4 0.0 copy-start.2
  53.4 0.0 copy-start.3
  53.4 1.4 second.1
  54.9 4.4 %collective-permute-start.1 = (f32[592,128]{1,0:T(8,128)S(1)}, f32[592,128]{1,0:T(8,128)S(1)}, u32[]{:S(2)}, u32[]{:S(2)}) collective-permute-start(f32[592,128]{1,0:T(8,128)S(1)} %get-tuple-element.24.sent), channel_id=1, source_target_pairs={{0,256},{256,0},{1,257},{257,1},{2,258},{258,2},{3,259},{259,3},{4... | collective-permute-start | bytes 909320 | tf_op jit(solution)/shard_map/ppermute | solution.py:301
  59.2 7.8 %collective-permute-done.1.got = f32[592,128]{1,0:T(8,128)S(1)} collective-permute-done((f32[592,128]{1,0:T(8,128)S(1)}, f32[592,128]{1,0:T(8,128)S(1)}, u32[]{:S(2)}, u32[]{:S(2)}) %collective-permute-start.1) | collective-permute-done | bytes 303136 | tf_op jit(solution)/shard_map/ppermute | solution.py:301
  67.0 1.5 %stats.1 = f32[32,8,128]{2,1,0:T(8,128)} custom-call(s32[3]{0:T(128)S(1)} %pad_add_fusion.place, f32[592,128]{1,0:T(8,128)S(1)} %get-tuple-element.25.kept, f32[592,128]{1,0:T(8,128)S(1)} %collective-permute-done.1.got), custom_call_target="tpu_custom_call" | custom-call | tf_op jit(solution)/shard_map/stats/pallas_call | solution.py:303
  68.5 7.5 %all-to-all-start.2 = ((f32[32,8,128]{2,1,0:T(8,128)}), f32[32,8,128]{2,1,0:T(8,128)S(1)}, u32[]{:S(2)}, u32[]{:S(2)}) async-start(f32[32,8,128]{2,1,0:T(8,128)} %stats.1), calls=%async_computation.2 | async-start | bytes 262144 | tf_op jit(solution)/shard_map/all_to_all | solution.py:306
  76.0 4.8 %collective-permute-start.2 = (f32[592,128]{1,0:T(8,128)S(1)}, f32[592,128]{1,0:T(8,128)S(1)}, u32[]{:S(2)}, u32[]{:S(2)}) collective-permute-start(f32[592,128]{1,0:T(8,128)S(1)} %get-tuple-element.25.kept), channel_id=1, source_target_pairs={{0,256},{256,0},{1,257},{257,1},{2,258},{258,2},{3,259},{259,3},{4... | collective-permute-start | bytes 909320 | tf_op jit(solution)/shard_map/ppermute | solution.py:305
  80.8 2.4 %all-to-all-done.2 = f32[32,8,128]{2,1,0:T(8,128)S(1)} async-done(((f32[32,8,128]{2,1,0:T(8,128)}), f32[32,8,128]{2,1,0:T(8,128)S(1)}, u32[]{:S(2)}, u32[]{:S(2)}) %all-to-all-start.2) | async-done | bytes 131104 | tf_op jit(solution)/shard_map/all_to_all | solution.py:306
  83.2 0.1 merge.1
  83.3 15.4 %all_to_all.31.tiles = f32[16,8,256]{2,1,0:T(8,128)S(1)} all-to-all(f32[16,8,256]{2,1,0:T(8,128)S(1)} %merge.1), channel_id=1, replica_groups=mesh['head'=2,'xlo'=2,'yhi'=4,'ylo'=2,'zhi'=4,'zlo'=2,'core'=2] {'yhi','..., dimensions={0} | all-to-all | bytes 262144 | tf_op jit(solution)/shard_map/all_to_all | solution.py:308
  98.7 0.1 final.1
  98.7 0.0 collective-permute-done.2.late
  98.7 0.0 copy-done.1
  98.7 0.0 copy-done.2
  98.7 0.0 copy-done.3
  98.8 3.2 %sent_part.1 = (bf16[256,640]{1,0:T(8,128)(2,1)S(1)}, bf16[256,2048]{1,0:T(8,128)(2,1)S(1)}) custom-call(s32[3]{0:T(128)S(1)} %pad_add_fusion.place, f32[592,128]{1,0:T(8,128)S(1)} %get-tuple-element.25.kept, f32[592,128]{1,0:T(8,128)S(1)} %collective-permute-done.1.got, f32[592,128]{1,0:T(8,128)S(1)} %get-tuple-element.24.sent, ...), custom_call_target="tpu_custom_call" | custom-call | tf_op jit(solution)/shard_map/sent_part/pallas_call | solution.py:314
  102.0 3.8 %collective-permute-start.3 = (bf16[256,2048]{1,0:T(8,128)(2,1)S(1)}, bf16[256,2048]{1,0:T(8,128)(2,1)S(1)}, u32[]{:S(2)}, u32[]{:S(2)}) collective-permute-start(bf16[256,2048]{1,0:T(8,128)(2,1)S(1)} %get-tuple-element.28), channel_id=1, source_target_pairs={{0,1},{1,0},{2,3},{3,2},{4,5},{5,4},{6,7},{7,6},{8,9},{9,8},{10,11... | collective-permute-start | bytes 3145736 | tf_op jit(solution)/shard_map/ppermute | solution.py:325
  105.8 2.7 %own.1.partial = f32[256,2048]{1,0:T(8,128)S(1)} custom-call(bf16[256,640]{1,0:T(8,128)(2,1)S(1)} %get-tuple-element.27.turned, bf16[592,2048]{1,0:T(8,128)(2,1)} %get-tuple-element.19.w_mine), custom_call_target="tpu_custom_call" | custom-call | tf_op jit(solution)/shard_map/own/pallas_call | solution.py:326
  108.5 0.0 collective-permute-done.3.back
  108.5 0.2 pair_sum.1
  108.7 17.7 %all_to_all.32 = bf16[8,256,256]{2,1,0:T(8,128)(2,1)S(1)} all-to-all(bf16[8,256,256]{2,1,0:T(8,128)(2,1)S(1)} %bitcast.17), channel_id=1, replica_groups=mesh['head'=2,'xlo'=2,'yhi'=4,'ylo'=2,'zhi'=4,'zlo'=2,'core'=2] {'xlo','..., dimensions={0} | all-to-all | bytes 2097152 | tf_op jit(solution)/shard_map/all_to_all | solution.py:266
  126.4 0.8 reduce_sum.21
  127.2 3.5 %all-to-all-start.5 = ((bf16[16,16,256]{2,1,0:T(8,128)(2,1)}), bf16[16,16,256]{2,1,0:T(8,128)(2,1)S(1)}, u32[]{:S(2)}, u32[]{:S(2)}) async-start(bf16[16,16,256]{2,1,0:T(8,128)(2,1)} %bitcast.11), calls=%async_computation.5 | async-start | bytes 262144 | tf_op jit(solution)/shard_map/all_to_all | solution.py:266
  130.7 0.6 fusion
  131.3 10.9 %all-to-all-done.5 = bf16[16,16,256]{2,1,0:T(8,128)(2,1)S(1)} async-done(((bf16[16,16,256]{2,1,0:T(8,128)(2,1)}), bf16[16,16,256]{2,1,0:T(8,128)(2,1)S(1)}, u32[]{:S(2)}, u32[]{:S(2)}) %all-to-all-start.5) | async-done | bytes 131104 | tf_op jit(solution)/shard_map/all_to_all | solution.py:266
  142.2 0.6 convert_reduce_fusion
Async XLA Ops:
  2.1 28.6 %all-to-all-start = ((bf16[32,16,256]{2,1,0:T(8,128)(2,1)}), bf16[32,16,256]{2,1,0:T(8,128)(2,1)S(1)}, u32[]{:S(2)}, u32[]{:S(2)}) async-start(bf16[32,16,256]{2,1,0:T(8,128)(2,1)} %broadcast_in_dim.4), calls=%async_computation | async-start | bytes 524288 | tf_op jit(solution)/shard_map/all_to_all | solution.py:260
  18.7 2.4 %copy-start = (bf16[4096,592]{0,1:T(8,128)(2,1)S(1)}, bf16[4096,592]{0,1:T(8,128)(2,1)}, u32[]{:S(2)}) copy-start(bf16[4096,592]{0,1:T(8,128)(2,1)} %param.6) | copy-start | bytes 14548996
  44.6 8.8 %collective-permute-start = (bf16[4,32,16,256]{3,2,1,0:T(8,128)(2,1)S(1)}, bf16[4,32,16,256]{3,2,1,0:T(8,128)(2,1)S(1)}, u32[]{:S(2)}, u32[]{:S(2)}) collective-permute-start(bf16[4,32,16,256]{3,2,1,0:T(8,128)(2,1)S(1)} %all_to_all.30), channel_id=1, source_target_pairs={{0,1},{1,0},{2,3},{3,2},{4,5},{5,4},{6,7},{7,6},{8,9},{9,8},{10,11... | collective-permute-start | bytes 3145736 | tf_op jit(solution)/shard_map/ppermute | solution.py:284
  53.4 45.3 %copy-start.1 = (s32[256]{0:T(256)S(1)}, s32[256]{0:T(256)}, u32[]{:S(2)}) copy-start(s32[256]{0:T(256)} %param.7) | copy-start | bytes 3076
  53.4 45.3 %copy-start.2 = (f32[256]{0:T(256)S(1)}, f32[256]{0:T(256)}, u32[]{:S(2)}) copy-start(f32[256]{0:T(256)} %param.8) | copy-start | bytes 3076
  53.4 45.3 %copy-start.3 = (f32[256]{0:T(256)S(1)}, f32[256]{0:T(256)}, u32[]{:S(2)}) copy-start(f32[256]{0:T(256)} %param.9) | copy-start | bytes 3076
  54.9 12.2 %collective-permute-start.1 = (f32[592,128]{1,0:T(8,128)S(1)}, f32[592,128]{1,0:T(8,128)S(1)}, u32[]{:S(2)}, u32[]{:S(2)}) collective-permute-start(f32[592,128]{1,0:T(8,128)S(1)} %get-tuple-element.24.sent), channel_id=1, source_target_pairs={{0,256},{256,0},{1,257},{257,1},{2,258},{258,2},{3,259},{259,3},{4... | collective-permute-start | bytes 909320 | tf_op jit(solution)/shard_map/ppermute | solution.py:301
  68.5 14.8 %all-to-all-start.2 = ((f32[32,8,128]{2,1,0:T(8,128)}), f32[32,8,128]{2,1,0:T(8,128)S(1)}, u32[]{:S(2)}, u32[]{:S(2)}) async-start(f32[32,8,128]{2,1,0:T(8,128)} %stats.1), calls=%async_computation.2 | async-start | bytes 262144 | tf_op jit(solution)/shard_map/all_to_all | solution.py:306
  76.0 22.7 %collective-permute-start.2 = (f32[592,128]{1,0:T(8,128)S(1)}, f32[592,128]{1,0:T(8,128)S(1)}, u32[]{:S(2)}, u32[]{:S(2)}) collective-permute-start(f32[592,128]{1,0:T(8,128)S(1)} %get-tuple-element.25.kept), channel_id=1, source_target_pairs={{0,256},{256,0},{1,257},{257,1},{2,258},{258,2},{3,259},{259,3},{4... | collective-permute-start | bytes 909320 | tf_op jit(solution)/shard_map/ppermute | solution.py:305
  102.0 6.5 %collective-permute-start.3 = (bf16[256,2048]{1,0:T(8,128)(2,1)S(1)}, bf16[256,2048]{1,0:T(8,128)(2,1)S(1)}, u32[]{:S(2)}, u32[]{:S(2)}) collective-permute-start(bf16[256,2048]{1,0:T(8,128)(2,1)S(1)} %get-tuple-element.28), channel_id=1, source_target_pairs={{0,1},{1,0},{2,3},{3,2},{4,5},{5,4},{6,7},{7,6},{8,9},{9,8},{10,11... | collective-permute-start | bytes 3145736 | tf_op jit(solution)/shard_map/ppermute | solution.py:325
  127.2 15.0 %all-to-all-start.5 = ((bf16[16,16,256]{2,1,0:T(8,128)(2,1)}), bf16[16,16,256]{2,1,0:T(8,128)(2,1)S(1)}, u32[]{:S(2)}, u32[]{:S(2)}) async-start(bf16[16,16,256]{2,1,0:T(8,128)(2,1)} %bitcast.11), calls=%async_computation.5 | async-start | bytes 262144 | tf_op jit(solution)/shard_map/all_to_all | solution.py:266

commit v4 on v3

--- a/solution.py
+++ b/solution.py
@@ -11,9 +11,8 @@
 Z = (ZHI, ZLO)
 NARROW = (*Z, CORE)
 WIDE = (HEAD, XLO, *Y)
-GATHER_FAR, GATHER_NEAR = (*Y, ZHI), (XLO, ZLO)
-STATS_NEAR, STATS_FAR = (HEAD, XLO, YLO, ZLO, CORE), (YHI, ZHI)
-REDUCE_NEAR, REDUCE_FAR = (XLO, YLO, ZLO), (YHI, ZHI)
+FAR = (XLO, YHI, ZHI)
+STATS_NEAR, STATS_FAR = NARROW, WIDE
 
 BETA = 0.2
 SWAP = [(0, 1), (1, 0)]
@@ -59,21 +58,30 @@
     )(place, weights)
 
 
-def fetch(sources, targets, sems):
-    copies = [
-        pltpu.make_async_copy(source, target, sems.at[k])
-        for k, (source, target) in enumerate(zip(sources, targets))
-    ]
+def fetch(sources, targets, sems, pieces=4):
+    copies = []
+    for k, (source, target) in enumerate(zip(sources, targets)):
+        tiles = source.shape[0] // STEP
+        for piece in range(pieces):
+            low, high = (STEP * (tiles * i // pieces) for i in (piece, piece + 1))
+            copies.append(
+                pltpu.make_async_copy(
+                    source.at[low:high], target.at[low:high], sems.at[k * pieces + piece]
+                )
+            )
     for copy in copies:
         copy.start()
     return copies
 
 
 def flatten(blocks, flat):
-    xlo, zlo, y, zhi, rows, width = blocks.shape
-    for z in range(zhi * zlo):
-        part = blocks[:, z % zlo, :, z // zlo].reshape(xlo * y * rows, width)
-        flat[:, z * width : (z + 1) * width] = part
+    ylo, zlo, xlo, yhi, zhi, rows, width = blocks.shape
+    for k in range(xlo * yhi * ylo):
+        x, y_hi, y_lo = k // (yhi * ylo), k // ylo % yhi, k % ylo
+        for z in range(zhi * zlo):
+            flat[k * rows : (k + 1) * rows, z * width : (z + 1) * width] = blocks[
+                y_lo, z % zlo, x, y_hi, z // zlo
+            ]
 
 
 def product(weights, flat):
@@ -85,9 +93,12 @@
 def first_kernel(mine, w_mine, w_other, out, next_weights, flat, here, sems):
     copies = fetch((w_mine, w_other), (here, next_weights), sems)
     flatten(mine, flat)
-    copies[0].wait()
+    half = len(copies) // 2
+    for copy in copies[:half]:
+        copy.wait()
     out[...] = product(here, flat)
-    copies[1].wait()
+    for copy in copies[half:]:
+        copy.wait()
 
 
 def second_kernel(place, part, other, weights, kept, sent, flat):
@@ -143,19 +154,16 @@
     return lse[0:1], cross, lse[2:3]
 
 
-def both_heads(tiles):
-    sides = [merged(tiles[k]) for k in range(2)]
-    return [jnp.concatenate(pair, 1) for pair in zip(*sides)]
-
-
 def merge_kernel(tiles, out):
-    out[...] = spread(both_heads(tiles), out.shape)
+    out[...] = spread(merged(tiles[...]), out.shape)
 
 
 def final_kernel(tiles, out):
-    policy_lse, cross, mixture_lse = merged(tiles[...])
-    lines = (policy_lse, cross - policy_lse + mixture_lse, mixture_lse)
-    out[...] = spread(lines, (1, *out.shape))[0]
+    half = tiles.shape[3]
+    for k in range(2):
+        policy_lse, cross, mixture_lse = merged(tiles[k])
+        lines = (policy_lse, cross - policy_lse + mixture_lse, mixture_lse)
+        out[:, k * half : (k + 1) * half] = spread(lines, (1, 8, half))[0]
 
 
 def sent_kernel(
@@ -207,7 +215,8 @@
     def _():
         fill((sent, late), (kept, got), False)
 
-    copies[0].wait()
+    for copy in copies:
+        copy.wait()
     for at, part in sums(turned, here):
         sent_out[:, at] = part.astype(bf16)
 
@@ -224,19 +233,20 @@
 
 def own_kernel(turned, w_mine, out, here, sems):
     copies = fetch((w_mine,), (here,), sems)
-    copies[0].wait()
+    for copy in copies:
+        copy.wait()
     for at, part in sums(turned, here):
         out[:, at] = part
 
 
 def pair_kernel(partial, back, out):
-    xlo, ylo, zlo, yhi, zhi, rows, width = out.shape
+    ylo, zlo, xlo, yhi, zhi, rows, width = out.shape
     for z in range(zhi * zlo):
         at = slice(z * width, (z + 1) * width)
         whole = (partial[:, at] + back[:, at].astype(f32)).astype(bf16)
         whole = whole.reshape(xlo, yhi, ylo, rows, width)
         for lo in range(ylo):
-            out[:, lo, z % zlo, :, z // zlo] = whole[:, :, lo]
+            out[lo, z % zlo, :, :, z // zlo] = whole[:, :, lo]
 
 
 def on_core(kernel, out_shape, count, name, scalars=True, scratch=(), hbm=0):
@@ -255,15 +265,33 @@
     return jax.ShapeDtypeStruct(shape, dtype)
 
 
-def copies(block, axes):
-    count = lax.axis_size(axes)
+def neighbours():
+    y_count, z_count, cores = (lax.axis_size(axes) for axes in (Y, Z, CORE))
+
+    def pairs(count, core):
+        for low in range(0, count, 2):
+            yield ((low + 2 * core) % count, low + 1)
+
+    return [
+        [(y * z_count + z) * cores + core for y in y_pair for z in z_pair]
+        for core in range(cores)
+        for y_pair in pairs(y_count, core)
+        for z_pair in pairs(z_count, core)
+    ]
+
+
+def swapped_near(parts):
     return lax.all_to_all(
-        jnp.broadcast_to(block[None], (count, *block.shape)), axes, 0, 0, tiled=True
-    )
-
-
-def exchange_sum(parts, axes):
-    return jnp.sum(lax.all_to_all(parts, axes, 0, 0, tiled=True).astype(f32), 0)
+        parts, (*Y, *Z, CORE), 0, 0, axis_index_groups=neighbours(), tiled=True
+    )
+
+
+def swapped_far(parts):
+    return lax.all_to_all(parts, FAR, 0, 0, tiled=True)
+
+
+def repeated(block, count):
+    return jnp.broadcast_to(block[None], (count, *block.shape))
 
 
 def body(hidden, head_weights, token_ids, kl_weight, advantage):
@@ -278,13 +306,14 @@
     w_mine, w_other = held(place, head_weights.T, depth)
     flat = [pltpu.VMEM((row_total, depth * width), bf16)]
 
-    far = copies(hidden, GATHER_FAR)
+    squares = ylo * zlo
+    far = swapped_far(repeated(hidden, lax.axis_size(FAR)))
     far, w_mine, w_other = lax.optimization_barrier((far, w_mine, w_other))
-    mine = copies(far, GATHER_NEAR)
+    mine = swapped_near(repeated(far, squares).reshape(-1, rows, width))
     other = lax.ppermute(mine, CORE, SWAP)
-    shape = (xlo, zlo, yhi * ylo, zhi, rows, width)
+    shape = (ylo, zlo, xlo, yhi, zhi, rows, width)
     w_half = array((columns, depth * width), bf16)
-    buffers = [pltpu.VMEM(w_half.shape, bf16), pltpu.SemaphoreType.DMA((2,))]
+    buffers = [pltpu.VMEM(w_half.shape, bf16), pltpu.SemaphoreType.DMA((8,))]
     part, w_next = on_core(
         first_kernel,
         [array((columns, row_total)), w_half],
@@ -303,9 +332,9 @@
     stats = on_core(stats_kernel, array((near, 8, half)), 2, "stats")(place, kept, got)
     kept_late, stats = lax.optimization_barrier((kept, stats))
     late = lax.ppermute(kept_late, HEAD, SWAP)
-    stats = lax.all_to_all(stats, STATS_NEAR, 0, 0, tiled=True).reshape(2, near // 2, 8, half)
-    stats = on_core(merge_kernel, array((far, 8, row_total)), 1, "merge", False)(stats)
-    stats = lax.all_to_all(stats, STATS_FAR, 0, 0, tiled=True)
+    stats = lax.all_to_all(stats, STATS_NEAR, 0, 0, tiled=True)
+    stats = on_core(merge_kernel, array((far, 8, half)), 1, "merge", False)(stats)
+    stats = lax.all_to_all(stats, STATS_FAR, 0, 0, tiled=True).reshape(2, far // 2, 8, half)
     final = on_core(final_kernel, array((8, row_total)), 1, "final", False)(stats)
 
     line = lambda a: a.reshape(1, row_total)
@@ -327,10 +356,11 @@
         turned, w_mine
     )
     pair_sum = on_core(
-        pair_kernel, array((xlo, ylo, zlo, yhi, zhi, rows, width), bf16), 2, "pair_sum", False
+        pair_kernel, array(shape, bf16), 2, "pair_sum", False
     )(partial, back)
-    near = exchange_sum(pair_sum.reshape(xlo * ylo * zlo, -1, width), REDUCE_NEAR).astype(bf16)
-    hidden_grad = exchange_sum(near.reshape(-1, rows, width), REDUCE_FAR).T
+    near = swapped_near(pair_sum.reshape(-1, rows, width)).reshape(squares, -1, rows, width)
+    near = jnp.sum(near.astype(f32), 0).astype(bf16)
+    hidden_grad = jnp.sum(swapped_far(near).astype(f32), 0).T
     return (hidden_grad, final[2], final[1])
 
 

time: 143 us -> 140 us (0.979)
  blocking collectives: 46.9 us -> 43.2 us
  waiting for transfers between devices: 27.8 us -> 30.8 us
  starting transfers between devices: 46.8 us -> 44.1 us
    all_to_all x3, blocking collectives: 46.9 us -> 43.2 us  [the longest x2 27.3 us: swapped_near(): lax.all_to_all(parts, (*Y, *Z, CORE), 0, 0, axis_index_groups=neighbours(...]
    ppermute x1, starting transfers between devices: 6.25 us -> 3.1 us  [body(): other = lax.ppermute(mine, CORE, SWAP)]
    all_to_all x3, waiting for transfers between devices: 20 us -> 23 us  [the longest x2 19.6 us: swapped_far(): return lax.all_to_all(parts, FAR, 0, 0, tiled=True)]
where the time goes in v4:
time: 140 us; the launch traced here: 139 us
  starting transfers between devices  44.1 us (32%)
  blocking collectives  43.2 us (31%)
  waiting for transfers between devices  30.8 us (22%)
  Pallas kernels  14.4 us (10%)
  local copies, waits for them, and re-layouts  4.47 us (3%)
  other arithmetic  1.63 us (1%)
    all_to_all x2, blocking collectives, swapped_near(): lax.all_to_all(parts, (*Y, *Z, CORE), 0, 0, axis_index_groups=neighbours(...  27.3 us
    all_to_all x2, starting transfers between devices, swapped_far(): return lax.all_to_all(parts, FAR, 0, 0, tiled=True)  23.4 us
    all_to_all x2, waiting for transfers between devices, swapped_far(): return lax.all_to_all(parts, FAR, 0, 0, tiled=True)  19.6 us
    all_to_all x1, blocking collectives, body(): lax.all_to_all(stats, STATS_FAR, 0, 0, tiled=True)  16 us
    ppermute x1, waiting for transfers between devices, body(): got = lax.ppermute(sent, HEAD, SWAP)  7.78 us
    all_to_all x1, starting transfers between devices, body(): stats = lax.all_to_all(stats, STATS_NEAR, 0, 0, tiled=True)  4.77 us
    ppermute x1, starting transfers between devices, body(): late = lax.ppermute(kept_late, HEAD, SWAP)  4.39 us
    ppermute x1, starting transfers between devices, body(): got = lax.ppermute(sent, HEAD, SWAP)  4.37 us
  transfers between devices with their start and end apart: 7, of which 4 were waited for; matrix products, arithmetic and copies ran while one was open for 0% of the time, Pallas kernels for 6%

profile of v4, /device:TPU:1, one launch (start us, length us, event | category | flops | bytes accessed | tf_op | source)
XLA Modules:
  0.0 139.4 jit_solution(7858698281880703581)
XLA Ops:
  0.6 1.4 %broadcast_in_dim.4 = bf16[32,16,256]{2,1,0:T(8,128)(2,1)} broadcast(bf16[16,256]{1,0:T(8,128)(2,1)} %param.5), dimensions={1,2} | broadcast | bytes 270336 | tf_op jit(solution)/shard_map/broadcast_in_dim | solution.py:294
  2.1 17.4 %all-to-all-start = ((bf16[32,16,256]{2,1,0:T(8,128)(2,1)}), bf16[32,16,256]{2,1,0:T(8,128)(2,1)S(1)}, u32[]{:S(2)}, u32[]{:S(2)}) async-start(bf16[32,16,256]{2,1,0:T(8,128)(2,1)} %broadcast_in_dim.4), calls=%async_computation | async-start | bytes 524288 | tf_op jit(solution)/shard_map/all_to_all | solution.py:290
  19.5 0.1 pad_add_fusion.place
  19.6 0.0 copy-start
  19.6 2.4 %copy-done = bf16[4096,592]{0,1:T(8,128)(2,1)S(1)} copy-done((bf16[4096,592]{0,1:T(8,128)(2,1)S(1)}, bf16[4096,592]{0,1:T(8,128)(2,1)}, u32[]{:S(2)}) %copy-start) | copy-done | bytes 4849688
  22.0 2.9 %hold.1 = (bf16[592,2048]{1,0:T(8,128)(2,1)}, bf16[592,2048]{1,0:T(8,128)(2,1)}) custom-call(s32[3]{0:T(128)S(1)} %pad_add_fusion.place, bf16[592,4096]{1,0:T(8,128)(2,1)S(1)} %bitcast.16), custom_call_target="tpu_custom_call" | custom-call | tf_op jit(solution)/shard_map/hold/pallas_call | solution.py:50
  24.8 7.6 %all-to-all-done = bf16[32,16,256]{2,1,0:T(8,128)(2,1)S(1)} async-done(((bf16[32,16,256]{2,1,0:T(8,128)(2,1)}), bf16[32,16,256]{2,1,0:T(8,128)(2,1)S(1)}, u32[]{:S(2)}, u32[]{:S(2)}) %all-to-all-start) | async-done | bytes 262176 | tf_op jit(solution)/shard_map/all_to_all | solution.py:290
  32.5 0.1 broadcast_in_dim.5
  32.6 13.6 %all_to_all.30 = bf16[128,16,256]{2,1,0:T(8,128)(2,1)S(1)} all-to-all(bf16[128,16,256]{2,1,0:T(8,128)(2,1)S(1)} %bitcast.24), channel_id=1, replica_groups={{0,2,16,18},{4,6,20,22},{8,10,24,26},{12,14,28,30},{32,34,48,50},{36,38..., dimensions={0} | all-to-all | bytes 2097152 | tf_op jit(solution)/shard_map/all_to_all | solution.py:284
  46.2 3.1 %collective-permute-start = (bf16[128,16,256]{2,1,0:T(8,128)(2,1)S(1)}, bf16[128,16,256]{2,1,0:T(8,128)(2,1)S(1)}, u32[]{:S(2)}, u32[]{:S(2)}) collective-permute-start(bf16[128,16,256]{2,1,0:T(8,128)(2,1)S(1)} %all_to_all.30), channel_id=1, source_target_pairs={{0,1},{1,0},{2,3},{3,2},{4,5},{5,4},{6,7},{7,6},{8,9},{9,8},{10,11... | collective-permute-start | bytes 3145736 | tf_op jit(solution)/shard_map/ppermute | solution.py:313
  49.3 2.5 %first.1 = (f32[592,256]{1,0:T(8,128)S(1)}, bf16[592,2048]{1,0:T(8,128)(2,1)S(1)}) custom-call(bf16[2,2,2,4,4,16,256]{6,5,4,3,2,1,0:T(8,128)(2,1)S(1)} %bitcast.17, bf16[592,2048]{1,0:T(8,128)(2,1)} %get-tuple-element.19.w_mine, bf16[592,2048]{1,0:T(8,128)(2,1)} %get-tuple-element.20.w_other), custom_call_target="tpu_custom_call" | custom-call | tf_op jit(solution)/shard_map/first/pallas_call | solution.py:317
  51.8 0.0 collective-permute-done
  51.8 0.0 copy-start.1
  51.9 0.0 copy-start.2
  51.9 0.0 copy-start.3
  51.9 1.4 %second.1 = (f32[592,128]{1,0:T(8,128)S(1)}, f32[592,128]{1,0:T(8,128)S(1)}) custom-call(s32[3]{0:T(128)S(1)} %pad_add_fusion.place, f32[592,256]{1,0:T(8,128)S(1)} %get-tuple-element.21.part, bf16[2,2,2,4,4,16,256]{6,5,4,3,2,1,0:T(8,128)(2,1)S(1)} %bitcast.19, bf16[592,2048]{1,0:T(8,128)(2,1)S(1)} %get-tuple-element.22.weights), custom_call_target="tpu_custom_call" | custom-call | tf_op jit(solution)/shard_map/second/pallas_call | solution.py:326
  53.3 4.4 %collective-permute-start.1 = (f32[592,128]{1,0:T(8,128)S(1)}, f32[592,128]{1,0:T(8,128)S(1)}, u32[]{:S(2)}, u32[]{:S(2)}) collective-permute-start(f32[592,128]{1,0:T(8,128)S(1)} %get-tuple-element.24.sent), channel_id=1, source_target_pairs={{0,256},{256,0},{1,257},{257,1},{2,258},{258,2},{3,259},{259,3},{4... | collective-permute-start | bytes 909320 | tf_op jit(solution)/shard_map/ppermute | solution.py:330
  57.7 7.8 %collective-permute-done.1.got = f32[592,128]{1,0:T(8,128)S(1)} collective-permute-done((f32[592,128]{1,0:T(8,128)S(1)}, f32[592,128]{1,0:T(8,128)S(1)}, u32[]{:S(2)}, u32[]{:S(2)}) %collective-permute-start.1) | collective-permute-done | bytes 303136 | tf_op jit(solution)/shard_map/ppermute | solution.py:330
  65.4 1.4 %stats.1 = f32[16,8,128]{2,1,0:T(8,128)} custom-call(s32[3]{0:T(128)S(1)} %pad_add_fusion.place, f32[592,128]{1,0:T(8,128)S(1)} %get-tuple-element.25.kept, f32[592,128]{1,0:T(8,128)S(1)} %collective-permute-done.1.got), custom_call_target="tpu_custom_call" | custom-call | tf_op jit(solution)/shard_map/stats/pallas_call | solution.py:332
  66.9 4.8 %all-to-all-start.2 = ((f32[16,8,128]{2,1,0:T(8,128)}), f32[16,8,128]{2,1,0:T(8,128)S(1)}, u32[]{:S(2)}, u32[]{:S(2)}) async-start(f32[16,8,128]{2,1,0:T(8,128)} %stats.1), calls=%async_computation.2 | async-start | bytes 131072 | tf_op jit(solution)/shard_map/all_to_all | solution.py:335
  71.6 4.4 %collective-permute-start.2 = (f32[592,128]{1,0:T(8,128)S(1)}, f32[592,128]{1,0:T(8,128)S(1)}, u32[]{:S(2)}, u32[]{:S(2)}) collective-permute-start(f32[592,128]{1,0:T(8,128)S(1)} %get-tuple-element.25.kept), channel_id=1, source_target_pairs={{0,256},{256,0},{1,257},{257,1},{2,258},{258,2},{3,259},{259,3},{4... | collective-permute-start | bytes 909320 | tf_op jit(solution)/shard_map/ppermute | solution.py:334
  76.0 3.4 %all-to-all-done.2.tiles = f32[16,8,128]{2,1,0:T(8,128)S(1)} async-done(((f32[16,8,128]{2,1,0:T(8,128)}), f32[16,8,128]{2,1,0:T(8,128)S(1)}, u32[]{:S(2)}, u32[]{:S(2)}) %all-to-all-start.2) | async-done | bytes 65568 | tf_op jit(solution)/shard_map/all_to_all | solution.py:335
  79.5 16.0 %all_to_all.31 = f32[32,8,128]{2,1,0:T(8,128)S(1)} all-to-all(f32[32,8,128]{2,1,0:T(8,128)S(1)} %merge.1), channel_id=1, replica_groups=mesh['head'=2,'xlo'=2,'yhi'=4,'ylo'=2,'zhi'=4,'zlo'=2,'core'=2] {'head',..., dimensions={0} | all-to-all | bytes 262144 | tf_op jit(solution)/shard_map/all_to_all | solution.py:337
  95.5 0.1 final.1
  95.5 0.0 collective-permute-done.2.late
  95.5 0.0 copy-done.1
  95.5 0.0 copy-done.2
  95.5 0.0 copy-done.3
  95.5 3.2 %sent_part.1 = (bf16[256,640]{1,0:T(8,128)(2,1)S(1)}, bf16[256,2048]{1,0:T(8,128)(2,1)S(1)}) custom-call(s32[3]{0:T(128)S(1)} %pad_add_fusion.place, f32[592,128]{1,0:T(8,128)S(1)} %get-tuple-element.25.kept, f32[592,128]{1,0:T(8,128)S(1)} %collective-permute-done.1.got, f32[592,128]{1,0:T(8,128)S(1)} %get-tuple-element.24.sent, ...), custom_call_target="tpu_custom_call" | custom-call | tf_op jit(solution)/shard_map/sent_part/pallas_call | solution.py:343
  98.8 4.0 %collective-permute-start.3 = (bf16[256,2048]{1,0:T(8,128)(2,1)S(1)}, bf16[256,2048]{1,0:T(8,128)(2,1)S(1)}, u32[]{:S(2)}, u32[]{:S(2)}) collective-permute-start(bf16[256,2048]{1,0:T(8,128)(2,1)S(1)} %get-tuple-element.28), channel_id=1, source_target_pairs={{0,1},{1,0},{2,3},{3,2},{4,5},{5,4},{6,7},{7,6},{8,9},{9,8},{10,11... | collective-permute-start | bytes 3145736 | tf_op jit(solution)/shard_map/ppermute | solution.py:354
  102.8 2.7 %own.1.partial = f32[256,2048]{1,0:T(8,128)S(1)} custom-call(bf16[256,640]{1,0:T(8,128)(2,1)S(1)} %get-tuple-element.27.turned, bf16[592,2048]{1,0:T(8,128)(2,1)} %get-tuple-element.19.w_mine), custom_call_target="tpu_custom_call" | custom-call | tf_op jit(solution)/shard_map/own/pallas_call | solution.py:355
  105.5 0.0 collective-permute-done.3.back
  105.5 0.2 pair_sum.1
  105.7 13.6 %all_to_all.32 = bf16[128,16,256]{2,1,0:T(8,128)(2,1)S(1)} all-to-all(bf16[128,16,256]{2,1,0:T(8,128)(2,1)S(1)} %bitcast.18), channel_id=1, replica_groups={{0,2,16,18},{4,6,20,22},{8,10,24,26},{12,14,28,30},{32,34,48,50},{36,38..., dimensions={0} | all-to-all | bytes 2097152 | tf_op jit(solution)/shard_map/all_to_all | solution.py:284
  119.3 0.9 reduce_sum.21
  120.2 6.0 %all-to-all-start.5 = ((bf16[32,16,256]{2,1,0:T(8,128)(2,1)}), bf16[32,16,256]{2,1,0:T(8,128)(2,1)S(1)}, u32[]{:S(2)}, u32[]{:S(2)}) async-start(bf16[32,16,256]{2,1,0:T(8,128)(2,1)} %reduce_sum.21), calls=%async_computation.5 | async-start | bytes 524288 | tf_op jit(solution)/shard_map/all_to_all | solution.py:290
  126.2 0.6 fusion
  126.8 11.9 %all-to-all-done.5 = bf16[32,16,256]{2,1,0:T(8,128)(2,1)S(1)} async-done(((bf16[32,16,256]{2,1,0:T(8,128)(2,1)}), bf16[32,16,256]{2,1,0:T(8,128)(2,1)S(1)}, u32[]{:S(2)}, u32[]{:S(2)}) %all-to-all-start.5) | async-done | bytes 262176 | tf_op jit(solution)/shard_map/all_to_all | solution.py:290
  138.7 0.7 convert_reduce_fusion
  (1 shorter events, 0.0 us)
Async XLA Ops:
  2.1 30.4 %all-to-all-start = ((bf16[32,16,256]{2,1,0:T(8,128)(2,1)}), bf16[32,16,256]{2,1,0:T(8,128)(2,1)S(1)}, u32[]{:S(2)}, u32[]{:S(2)}) async-start(bf16[32,16,256]{2,1,0:T(8,128)(2,1)} %broadcast_in_dim.4), calls=%async_computation | async-start | bytes 524288 | tf_op jit(solution)/shard_map/all_to_all | solution.py:290
  19.6 2.4 %copy-start = (bf16[4096,592]{0,1:T(8,128)(2,1)S(1)}, bf16[4096,592]{0,1:T(8,128)(2,1)}, u32[]{:S(2)}) copy-start(bf16[4096,592]{0,1:T(8,128)(2,1)} %param.6) | copy-start | bytes 14548996
  46.2 5.6 %collective-permute-start = (bf16[128,16,256]{2,1,0:T(8,128)(2,1)S(1)}, bf16[128,16,256]{2,1,0:T(8,128)(2,1)S(1)}, u32[]{:S(2)}, u32[]{:S(2)}) collective-permute-start(bf16[128,16,256]{2,1,0:T(8,128)(2,1)S(1)} %all_to_all.30), channel_id=1, source_target_pairs={{0,1},{1,0},{2,3},{3,2},{4,5},{5,4},{6,7},{7,6},{8,9},{9,8},{10,11... | collective-permute-start | bytes 3145736 | tf_op jit(solution)/shard_map/ppermute | solution.py:313
  51.8 43.7 %copy-start.1 = (s32[256]{0:T(256)S(1)}, s32[256]{0:T(256)}, u32[]{:S(2)}) copy-start(s32[256]{0:T(256)} %param.7) | copy-start | bytes 3076
  51.9 43.7 %copy-start.2 = (f32[256]{0:T(256)S(1)}, f32[256]{0:T(256)}, u32[]{:S(2)}) copy-start(f32[256]{0:T(256)} %param.8) | copy-start | bytes 3076
  51.9 43.7 %copy-start.3 = (f32[256]{0:T(256)S(1)}, f32[256]{0:T(256)}, u32[]{:S(2)}) copy-start(f32[256]{0:T(256)} %param.9) | copy-start | bytes 3076
  53.3 12.2 %collective-permute-start.1 = (f32[592,128]{1,0:T(8,128)S(1)}, f32[592,128]{1,0:T(8,128)S(1)}, u32[]{:S(2)}, u32[]{:S(2)}) collective-permute-start(f32[592,128]{1,0:T(8,128)S(1)} %get-tuple-element.24.sent), channel_id=1, source_target_pairs={{0,256},{256,0},{1,257},{257,1},{2,258},{258,2},{3,259},{259,3},{4... | collective-permute-start | bytes 909320 | tf_op jit(solution)/shard_map/ppermute | solution.py:330
  66.9 12.6 %all-to-all-start.2 = ((f32[16,8,128]{2,1,0:T(8,128)}), f32[16,8,128]{2,1,0:T(8,128)S(1)}, u32[]{:S(2)}, u32[]{:S(2)}) async-start(f32[16,8,128]{2,1,0:T(8,128)} %stats.1), calls=%async_computation.2 | async-start | bytes 131072 | tf_op jit(solution)/shard_map/all_to_all | solution.py:335
  71.6 23.9 %collective-permute-start.2 = (f32[592,128]{1,0:T(8,128)S(1)}, f32[592,128]{1,0:T(8,128)S(1)}, u32[]{:S(2)}, u32[]{:S(2)}) collective-permute-start(f32[592,128]{1,0:T(8,128)S(1)} %get-tuple-element.25.kept), channel_id=1, source_target_pairs={{0,256},{256,0},{1,257},{257,1},{2,258},{258,2},{3,259},{259,3},{4... | collective-permute-start | bytes 909320 | tf_op jit(solution)/shard_map/ppermute | solution.py:334
  98.8 6.7 %collective-permute-start.3 = (bf16[256,2048]{1,0:T(8,128)(2,1)S(1)}, bf16[256,2048]{1,0:T(8,128)(2,1)S(1)}, u32[]{:S(2)}, u32[]{:S(2)}) collective-permute-start(bf16[256,2048]{1,0:T(8,128)(2,1)S(1)} %get-tuple-element.28), channel_id=1, source_target_pairs={{0,1},{1,0},{2,3},{3,2},{4,5},{5,4},{6,7},{7,6},{8,9},{9,8},{10,11... | collective-permute-start | bytes 3145736 | tf_op jit(solution)/shard_map/ppermute | solution.py:354
  120.2 18.5 %all-to-all-start.5 = ((bf16[32,16,256]{2,1,0:T(8,128)(2,1)}), bf16[32,16,256]{2,1,0:T(8,128)(2,1)S(1)}, u32[]{:S(2)}, u32[]{:S(2)}) async-start(bf16[32,16,256]{2,1,0:T(8,128)(2,1)} %reduce_sum.21), calls=%async_computation.5 | async-start | bytes 524288 | tf_op jit(solution)/shard_map/all_to_all | solution.py:290

commit v5 on v4

--- a/solution.py
+++ b/solution.py
@@ -12,7 +12,7 @@
 NARROW = (*Z, CORE)
 WIDE = (HEAD, XLO, *Y)
 FAR = (XLO, YHI, ZHI)
-STATS_NEAR, STATS_FAR = NARROW, WIDE
+STATS_NEAR, STATS_FAR = (*Y, CORE), (HEAD, XLO, *Z)
 
 BETA = 0.2
 SWAP = [(0, 1), (1, 0)]
@@ -158,12 +158,15 @@
     out[...] = spread(merged(tiles[...]), out.shape)
 
 
-def final_kernel(tiles, out):
+def final_kernel(tiles, out, lse_out, divergence_out):
     half = tiles.shape[3]
     for k in range(2):
         policy_lse, cross, mixture_lse = merged(tiles[k])
-        lines = (policy_lse, cross - policy_lse + mixture_lse, mixture_lse)
-        out[:, k * half : (k + 1) * half] = spread(lines, (1, 8, half))[0]
+        divergence = cross - policy_lse + mixture_lse
+        at = slice(k * half, (k + 1) * half)
+        out[:, at] = spread((policy_lse, divergence, mixture_lse), (1, 8, half))[0]
+        lse_out[:, at] = mixture_lse
+        divergence_out[:, at] = divergence
 
 
 def sent_kernel(
@@ -335,7 +338,9 @@
     stats = lax.all_to_all(stats, STATS_NEAR, 0, 0, tiled=True)
     stats = on_core(merge_kernel, array((far, 8, half)), 1, "merge", False)(stats)
     stats = lax.all_to_all(stats, STATS_FAR, 0, 0, tiled=True).reshape(2, far // 2, 8, half)
-    final = on_core(final_kernel, array((8, row_total)), 1, "final", False)(stats)
+    final, mixture_lse, divergence = on_core(
+        final_kernel, [array((n, row_total)) for n in (8, 1, 1)], 1, "final", False
+    )(stats)
 
     line = lambda a: a.reshape(1, row_total)
     padded = -(-columns // LANES) * LANES
@@ -361,7 +366,7 @@
     near = swapped_near(pair_sum.reshape(-1, rows, width)).reshape(squares, -1, rows, width)
     near = jnp.sum(near.astype(f32), 0).astype(bf16)
     hidden_grad = jnp.sum(swapped_far(near).astype(f32), 0).T
-    return (hidden_grad, final[2], final[1])
+    return (hidden_grad, mixture_lse.reshape(row_total), divergence.reshape(row_total))
 
 
 def solution(mesh):

time: 140 us -> 140 us (level)
  blocking collectives: 43.2 us -> 60.4 us
  waiting for transfers between devices: 30.8 us -> 18.8 us
  starting transfers between devices: 44.1 us -> 39.2 us
    all_to_all x0 -> x1, blocking collectives: none -> 18.3 us  [swapped_far(): return lax.all_to_all(parts, FAR, 0, 0, tiled=True)]
    all_to_all x2 -> x1, waiting for transfers between devices: 19.6 us -> 7.62 us  [swapped_far(): return lax.all_to_all(parts, FAR, 0, 0, tiled=True)]
    all_to_all x2 -> x1, starting transfers between devices: 23.4 us -> 17.4 us  [swapped_far(): return lax.all_to_all(parts, FAR, 0, 0, tiled=True)]
  transfers between devices with their start and end apart: 7 -> 6, of which waited for: 4 -> 3; matrix products, arithmetic and copies ran while one was open for 0% -> 0% of each run, Pallas kernels for 6% -> 6%
where the time goes in v5:
time: 140 us; the launch traced here: 139 us
  blocking collectives  60.4 us (43%)
  starting transfers between devices  39.2 us (28%)
  waiting for transfers between devices  18.8 us (13%)
  Pallas kernels  15 us (11%)
  local copies, waits for them, and re-layouts  3.89 us (3%)
    all_to_all x2, blocking collectives, swapped_near(): lax.all_to_all(parts, (*Y, *Z, CORE), 0, 0, axis_index_groups=neighbours(...  27.3 us
    all_to_all x1, blocking collectives, swapped_far(): return lax.all_to_all(parts, FAR, 0, 0, tiled=True)  18.3 us
    all_to_all x1, starting transfers between devices, swapped_far(): return lax.all_to_all(parts, FAR, 0, 0, tiled=True)  17.4 us
    all_to_all x1, blocking collectives, body(): lax.all_to_all(stats, STATS_FAR, 0, 0, tiled=True)  14.9 us
    ppermute x1, waiting for transfers between devices, body(): got = lax.ppermute(sent, HEAD, SWAP)  7.78 us
    all_to_all x1, waiting for transfers between devices, swapped_far(): return lax.all_to_all(parts, FAR, 0, 0, tiled=True)  7.62 us
    all_to_all x1, starting transfers between devices, body(): stats = lax.all_to_all(stats, STATS_NEAR, 0, 0, tiled=True)  5.87 us
    ppermute x1, starting transfers between devices, body(): late = lax.ppermute(kept_late, HEAD, SWAP)  4.4 us
  transfers between devices with their start and end apart: 6, of which 3 were waited for; matrix products, arithmetic and copies ran while one was open for 0% of the time, Pallas kernels for 6%

profile of v5, /device:TPU:1, one launch (start us, length us, event | category | flops | bytes accessed | tf_op | source)
XLA Modules:
  0.0 139.1 jit_solution(93727584061368213)
XLA Ops:
  0.6 1.4 %broadcast_in_dim.4 = bf16[32,16,256]{2,1,0:T(8,128)(2,1)} broadcast(bf16[16,256]{1,0:T(8,128)(2,1)} %param.5), dimensions={1,2} | broadcast | bytes 270336 | tf_op jit(solution)/shard_map/broadcast_in_dim | solution.py:297
  2.1 17.4 %all-to-all-start = ((bf16[32,16,256]{2,1,0:T(8,128)(2,1)}), bf16[32,16,256]{2,1,0:T(8,128)(2,1)S(1)}, u32[]{:S(2)}, u32[]{:S(2)}) async-start(bf16[32,16,256]{2,1,0:T(8,128)(2,1)} %broadcast_in_dim.4), calls=%async_computation | async-start | bytes 524288 | tf_op jit(solution)/shard_map/all_to_all | solution.py:293
  19.5 0.1 pad_add_fusion.place
  19.6 0.0 copy-start
  19.6 2.4 %copy-done = bf16[4096,592]{0,1:T(8,128)(2,1)S(1)} copy-done((bf16[4096,592]{0,1:T(8,128)(2,1)S(1)}, bf16[4096,592]{0,1:T(8,128)(2,1)}, u32[]{:S(2)}) %copy-start) | copy-done | bytes 4849688
  22.0 2.9 %hold.1 = (bf16[592,2048]{1,0:T(8,128)(2,1)}, bf16[592,2048]{1,0:T(8,128)(2,1)}) custom-call(s32[3]{0:T(128)S(1)} %pad_add_fusion.place, bf16[592,4096]{1,0:T(8,128)(2,1)S(1)} %bitcast.16), custom_call_target="tpu_custom_call" | custom-call | tf_op jit(solution)/shard_map/hold/pallas_call | solution.py:50
  24.9 7.6 %all-to-all-done = bf16[32,16,256]{2,1,0:T(8,128)(2,1)S(1)} async-done(((bf16[32,16,256]{2,1,0:T(8,128)(2,1)}), bf16[32,16,256]{2,1,0:T(8,128)(2,1)S(1)}, u32[]{:S(2)}, u32[]{:S(2)}) %all-to-all-start) | async-done | bytes 262176 | tf_op jit(solution)/shard_map/all_to_all | solution.py:293
  32.5 0.1 broadcast_in_dim.5
  32.6 13.6 %all_to_all.30 = bf16[128,16,256]{2,1,0:T(8,128)(2,1)S(1)} all-to-all(bf16[128,16,256]{2,1,0:T(8,128)(2,1)S(1)} %bitcast.24), channel_id=1, replica_groups={{0,2,16,18},{4,6,20,22},{8,10,24,26},{12,14,28,30},{32,34,48,50},{36,38..., dimensions={0} | all-to-all | bytes 2097152 | tf_op jit(solution)/shard_map/all_to_all | solution.py:287
  46.2 3.1 %collective-permute-start = (bf16[128,16,256]{2,1,0:T(8,128)(2,1)S(1)}, bf16[128,16,256]{2,1,0:T(8,128)(2,1)S(1)}, u32[]{:S(2)}, u32[]{:S(2)}) collective-permute-start(bf16[128,16,256]{2,1,0:T(8,128)(2,1)S(1)} %all_to_all.30), channel_id=1, source_target_pairs={{0,1},{1,0},{2,3},{3,2},{4,5},{5,4},{6,7},{7,6},{8,9},{9,8},{10,11... | collective-permute-start | bytes 3145736 | tf_op jit(solution)/shard_map/ppermute | solution.py:316
  49.3 2.5 %first.1 = (f32[592,256]{1,0:T(8,128)S(1)}, bf16[592,2048]{1,0:T(8,128)(2,1)S(1)}) custom-call(bf16[2,2,2,4,4,16,256]{6,5,4,3,2,1,0:T(8,128)(2,1)S(1)} %bitcast.17, bf16[592,2048]{1,0:T(8,128)(2,1)} %get-tuple-element.22.w_mine, bf16[592,2048]{1,0:T(8,128)(2,1)} %get-tuple-element.23.w_other), custom_call_target="tpu_custom_call" | custom-call | tf_op jit(solution)/shard_map/first/pallas_call | solution.py:320
  51.8 0.0 collective-permute-done
  51.8 0.0 copy-start.1
  51.9 0.0 copy-start.2
  51.9 0.0 copy-start.3
  51.9 1.4 %second.1 = (f32[592,128]{1,0:T(8,128)S(1)}, f32[592,128]{1,0:T(8,128)S(1)}) custom-call(s32[3]{0:T(128)S(1)} %pad_add_fusion.place, f32[592,256]{1,0:T(8,128)S(1)} %get-tuple-element.24.part, bf16[2,2,2,4,4,16,256]{6,5,4,3,2,1,0:T(8,128)(2,1)S(1)} %bitcast.19, bf16[592,2048]{1,0:T(8,128)(2,1)S(1)} %get-tuple-element.25.weights), custom_call_target="tpu_custom_call" | custom-call | tf_op jit(solution)/shard_map/second/pallas_call | solution.py:329
  53.3 4.4 %collective-permute-start.1 = (f32[592,128]{1,0:T(8,128)S(1)}, f32[592,128]{1,0:T(8,128)S(1)}, u32[]{:S(2)}, u32[]{:S(2)}) collective-permute-start(f32[592,128]{1,0:T(8,128)S(1)} %get-tuple-element.27.sent), channel_id=1, source_target_pairs={{0,256},{256,0},{1,257},{257,1},{2,258},{258,2},{3,259},{259,3},{4... | collective-permute-start | bytes 909320 | tf_op jit(solution)/shard_map/ppermute | solution.py:333
  57.7 7.8 %collective-permute-done.1.got = f32[592,128]{1,0:T(8,128)S(1)} collective-permute-done((f32[592,128]{1,0:T(8,128)S(1)}, f32[592,128]{1,0:T(8,128)S(1)}, u32[]{:S(2)}, u32[]{:S(2)}) %collective-permute-start.1) | collective-permute-done | bytes 303136 | tf_op jit(solution)/shard_map/ppermute | solution.py:333
  65.4 1.4 %stats.1 = f32[16,8,128]{2,1,0:T(8,128)} custom-call(s32[3]{0:T(128)S(1)} %pad_add_fusion.place, f32[592,128]{1,0:T(8,128)S(1)} %get-tuple-element.28.kept, f32[592,128]{1,0:T(8,128)S(1)} %collective-permute-done.1.got), custom_call_target="tpu_custom_call" | custom-call | tf_op jit(solution)/shard_map/stats/pallas_call | solution.py:335
  66.9 5.9 %all-to-all-start.2 = ((f32[16,8,128]{2,1,0:T(8,128)}), f32[16,8,128]{2,1,0:T(8,128)S(1)}, u32[]{:S(2)}, u32[]{:S(2)}) async-start(f32[16,8,128]{2,1,0:T(8,128)} %stats.1), calls=%async_computation.2 | async-start | bytes 131072 | tf_op jit(solution)/shard_map/all_to_all | solution.py:338
  72.7 4.4 %collective-permute-start.2 = (f32[592,128]{1,0:T(8,128)S(1)}, f32[592,128]{1,0:T(8,128)S(1)}, u32[]{:S(2)}, u32[]{:S(2)}) collective-permute-start(f32[592,128]{1,0:T(8,128)S(1)} %get-tuple-element.28.kept), channel_id=1, source_target_pairs={{0,256},{256,0},{1,257},{257,1},{2,258},{258,2},{3,259},{259,3},{4... | collective-permute-start | bytes 909320 | tf_op jit(solution)/shard_map/ppermute | solution.py:337
  77.1 3.4 %all-to-all-done.2.tiles = f32[16,8,128]{2,1,0:T(8,128)S(1)} async-done(((f32[16,8,128]{2,1,0:T(8,128)}), f32[16,8,128]{2,1,0:T(8,128)S(1)}, u32[]{:S(2)}, u32[]{:S(2)}) %all-to-all-start.2) | async-done | bytes 65568 | tf_op jit(solution)/shard_map/all_to_all | solution.py:338
  80.6 14.9 %all_to_all.31 = f32[32,8,128]{2,1,0:T(8,128)S(1)} all-to-all(f32[32,8,128]{2,1,0:T(8,128)S(1)} %merge.1), channel_id=1, replica_groups=mesh['head'=2,'xlo'=2,'yhi'=4,'ylo'=2,'zhi'=4,'zlo'=2,'core'=2] {'head',..., dimensions={0} | all-to-all | bytes 262144 | tf_op jit(solution)/shard_map/all_to_all | solution.py:340
  95.5 0.6 final.1
  96.1 0.0 collective-permute-done.2.late
  96.1 0.0 copy-done.1
  96.1 0.0 copy-done.2
  96.1 0.0 copy-done.3
  96.1 3.2 %sent_part.1 = (bf16[256,640]{1,0:T(8,128)(2,1)S(1)}, bf16[256,2048]{1,0:T(8,128)(2,1)S(1)}) custom-call(s32[3]{0:T(128)S(1)} %pad_add_fusion.place, f32[592,128]{1,0:T(8,128)S(1)} %get-tuple-element.28.kept, f32[592,128]{1,0:T(8,128)S(1)} %collective-permute-done.1.got, f32[592,128]{1,0:T(8,128)S(1)} %get-tuple-element.27.sent, ...), custom_call_target="tpu_custom_call" | custom-call | tf_op jit(solution)/shard_map/sent_part/pallas_call | solution.py:348
  99.3 4.0 %collective-permute-start.3 = (bf16[256,2048]{1,0:T(8,128)(2,1)S(1)}, bf16[256,2048]{1,0:T(8,128)(2,1)S(1)}, u32[]{:S(2)}, u32[]{:S(2)}) collective-permute-start(bf16[256,2048]{1,0:T(8,128)(2,1)S(1)} %get-tuple-element.32), channel_id=1, source_target_pairs={{0,1},{1,0},{2,3},{3,2},{4,5},{5,4},{6,7},{7,6},{8,9},{9,8},{10,11... | collective-permute-start | bytes 3145736 | tf_op jit(solution)/shard_map/ppermute | solution.py:359
  103.3 2.7 %own.1.partial = f32[256,2048]{1,0:T(8,128)S(1)} custom-call(bf16[256,640]{1,0:T(8,128)(2,1)S(1)} %get-tuple-element.31.turned, bf16[592,2048]{1,0:T(8,128)(2,1)} %get-tuple-element.22.w_mine), custom_call_target="tpu_custom_call" | custom-call | tf_op jit(solution)/shard_map/own/pallas_call | solution.py:360
  106.0 0.0 collective-permute-done.3.back
  106.0 0.2 pair_sum.1
  106.3 13.6 %all_to_all.32 = bf16[128,16,256]{2,1,0:T(8,128)(2,1)S(1)} all-to-all(bf16[128,16,256]{2,1,0:T(8,128)(2,1)S(1)} %bitcast.18), channel_id=1, replica_groups={{0,2,16,18},{4,6,20,22},{8,10,24,26},{12,14,28,30},{32,34,48,50},{36,38..., dimensions={0} | all-to-all | bytes 2097152 | tf_op jit(solution)/shard_map/all_to_all | solution.py:287
  119.9 0.2 reduce_sum.21
  120.1 18.3 %all_to_all.33 = bf16[32,16,256]{2,1,0:T(8,128)(2,1)S(1)} all-to-all(bf16[32,16,256]{2,1,0:T(8,128)(2,1)S(1)} %reduce_sum.21), channel_id=1, replica_groups=mesh['head'=2,'xlo'=2,'yhi'=4,'ylo'=2,'zhi'=4,'zlo'=2,'core'=2] {'xlo','..., dimensions={0} | all-to-all | bytes 524288 | tf_op jit(solution)/shard_map/all_to_all | solution.py:293
  138.4 0.7 convert_reduce_fusion
  (1 shorter events, 0.0 us)
Async XLA Ops:
  2.1 30.4 %all-to-all-start = ((bf16[32,16,256]{2,1,0:T(8,128)(2,1)}), bf16[32,16,256]{2,1,0:T(8,128)(2,1)S(1)}, u32[]{:S(2)}, u32[]{:S(2)}) async-start(bf16[32,16,256]{2,1,0:T(8,128)(2,1)} %broadcast_in_dim.4), calls=%async_computation | async-start | bytes 524288 | tf_op jit(solution)/shard_map/all_to_all | solution.py:293
  19.6 2.4 %copy-start = (bf16[4096,592]{0,1:T(8,128)(2,1)S(1)}, bf16[4096,592]{0,1:T(8,128)(2,1)}, u32[]{:S(2)}) copy-start(bf16[4096,592]{0,1:T(8,128)(2,1)} %param.6) | copy-start | bytes 14548996
  46.2 5.6 %collective-permute-start = (bf16[128,16,256]{2,1,0:T(8,128)(2,1)S(1)}, bf16[128,16,256]{2,1,0:T(8,128)(2,1)S(1)}, u32[]{:S(2)}, u32[]{:S(2)}) collective-permute-start(bf16[128,16,256]{2,1,0:T(8,128)(2,1)S(1)} %all_to_all.30), channel_id=1, source_target_pairs={{0,1},{1,0},{2,3},{3,2},{4,5},{5,4},{6,7},{7,6},{8,9},{9,8},{10,11... | collective-permute-start | bytes 3145736 | tf_op jit(solution)/shard_map/ppermute | solution.py:316
  51.8 44.2 %copy-start.1 = (s32[256]{0:T(256)S(1)}, s32[256]{0:T(256)}, u32[]{:S(2)}) copy-start(s32[256]{0:T(256)} %param.7) | copy-start | bytes 3076
  51.9 44.2 %copy-start.2 = (f32[256]{0:T(256)S(1)}, f32[256]{0:T(256)}, u32[]{:S(2)}) copy-start(f32[256]{0:T(256)} %param.8) | copy-start | bytes 3076
  51.9 44.2 %copy-start.3 = (f32[256]{0:T(256)S(1)}, f32[256]{0:T(256)}, u32[]{:S(2)}) copy-start(f32[256]{0:T(256)} %param.9) | copy-start | bytes 3076
  53.3 12.2 %collective-permute-start.1 = (f32[592,128]{1,0:T(8,128)S(1)}, f32[592,128]{1,0:T(8,128)S(1)}, u32[]{:S(2)}, u32[]{:S(2)}) collective-permute-start(f32[592,128]{1,0:T(8,128)S(1)} %get-tuple-element.27.sent), channel_id=1, source_target_pairs={{0,256},{256,0},{1,257},{257,1},{2,258},{258,2},{3,259},{259,3},{4... | collective-permute-start | bytes 909320 | tf_op jit(solution)/shard_map/ppermute | solution.py:333
  66.9 13.7 %all-to-all-start.2 = ((f32[16,8,128]{2,1,0:T(8,128)}), f32[16,8,128]{2,1,0:T(8,128)S(1)}, u32[]{:S(2)}, u32[]{:S(2)}) async-start(f32[16,8,128]{2,1,0:T(8,128)} %stats.1), calls=%async_computation.2 | async-start | bytes 131072 | tf_op jit(solution)/shard_map/all_to_all | solution.py:338
  72.7 23.4 %collective-permute-start.2 = (f32[592,128]{1,0:T(8,128)S(1)}, f32[592,128]{1,0:T(8,128)S(1)}, u32[]{:S(2)}, u32[]{:S(2)}) collective-permute-start(f32[592,128]{1,0:T(8,128)S(1)} %get-tuple-element.28.kept), channel_id=1, source_target_pairs={{0,256},{256,0},{1,257},{257,1},{2,258},{258,2},{3,259},{259,3},{4... | collective-permute-start | bytes 909320 | tf_op jit(solution)/shard_map/ppermute | solution.py:337
  99.3 6.7 %collective-permute-start.3 = (bf16[256,2048]{1,0:T(8,128)(2,1)S(1)}, bf16[256,2048]{1,0:T(8,128)(2,1)S(1)}, u32[]{:S(2)}, u32[]{:S(2)}) collective-permute-start(bf16[256,2048]{1,0:T(8,128)(2,1)S(1)} %get-tuple-element.32), channel_id=1, source_target_pairs={{0,1},{1,0},{2,3},{3,2},{4,5},{5,4},{6,7},{7,6},{8,9},{9,8},{10,11... | collective-permute-start | bytes 3145736 | tf_op jit(solution)/shard_map/ppermute | solution.py:359

commit v6 on v5

--- a/solution.py
+++ b/solution.py
@@ -171,9 +171,8 @@
 
 def sent_kernel(
     place, kept, got, sent, late, final, ids, kl_weight, advantage, w_other,
-    turned, sent_out, flat, here, sems,
+    turned, sent_out, flat,
 ):
-    copies = fetch((w_other,), (here,), sems)
     columns, half = kept.shape
     padded = flat.shape[0]
 
@@ -218,10 +217,13 @@
     def _():
         fill((sent, late), (kept, got), False)
 
-    for copy in copies:
-        copy.wait()
-    for at, part in sums(turned, here):
+    for at, part in sums(turned, w_other):
         sent_out[:, at] = part.astype(bf16)
+
+
+def fetch_kernel(weights, out, sems):
+    for copy in fetch((weights,), (out,), sems):
+        copy.wait()
 
 
 def sums(turned, weights, step=512):
@@ -333,9 +335,13 @@
     got = lax.ppermute(sent, HEAD, SWAP)
     near, far = lax.axis_size(STATS_NEAR), lax.axis_size(STATS_FAR)
     stats = on_core(stats_kernel, array((near, 8, half)), 2, "stats")(place, kept, got)
-    kept_late, stats = lax.optimization_barrier((kept, stats))
+    kept_late, stats, w_other = lax.optimization_barrier((kept, stats, w_other))
     late = lax.ppermute(kept_late, HEAD, SWAP)
+    w_near = on_core(
+        fetch_kernel, w_half, 0, "fetch", False, scratch=buffers[1:], hbm=1
+    )(w_other)
     stats = lax.all_to_all(stats, STATS_NEAR, 0, 0, tiled=True)
+    stats, w_near = lax.optimization_barrier((stats, w_near))
     stats = on_core(merge_kernel, array((far, 8, half)), 1, "merge", False)(stats)
     stats = lax.all_to_all(stats, STATS_FAR, 0, 0, tiled=True).reshape(2, far // 2, 8, half)
     final, mixture_lse, divergence = on_core(
@@ -348,13 +354,12 @@
     turned, sent_part = on_core(
         sent_kernel,
         [array((row_total, padded), bf16), array(wide_rows, bf16)],
-        8,
+        9,
         "sent_part",
-        scratch=[pltpu.VMEM((padded, row_total), f32), *buffers],
-        hbm=1,
+        scratch=[pltpu.VMEM((padded, row_total), f32)],
     )(
         place, kept, got, sent, late, final, line(token_ids), line(kl_weight), line(advantage),
-        w_other,
+        w_near,
     )
     back = lax.ppermute(sent_part, CORE, SWAP)
     partial = on_core(own_kernel, array(wide_rows), 1, "own", False, scratch=buffers, hbm=1)(

time: 140 us -> 139 us (level)
  waiting for transfers between devices: 18.8 us -> 16.9 us
    all_to_all x1, waiting for transfers between devices: 3.4 us -> 1.53 us  [body(): stats = lax.all_to_all(stats, STATS_NEAR, 0, 0, tiled=True)]
    pallas_call x0 -> x1, Pallas kernels: none -> 1.69 us  [body(): on_core(fetch_kernel, w_half, 0, 'fetch', False, scratch=buffers[1:], hbm=1)]
  transfers between devices with their start and end apart: 6 -> 6, of which waited for: 3 -> 3; matrix products, arithmetic and copies ran while one was open for 0% -> 0% of each run, Pallas kernels for 6% -> 8%
where the time goes in v6:
time: 139 us
  blocking collectives  60.6 us (44%)
  starting transfers between devices  39.4 us (28%)
  waiting for transfers between devices  16.9 us (12%)
  Pallas kernels  16 us (12%)
  local copies, waits for them, and re-layouts  3.89 us (3%)
    all_to_all x2, blocking collectives, swapped_near(): lax.all_to_all(parts, (*Y, *Z, CORE), 0, 0, axis_index_groups=neighbours(...  27.3 us
    all_to_all x1, blocking collectives, swapped_far(): return lax.all_to_all(parts, FAR, 0, 0, tiled=True)  18.5 us
    all_to_all x1, starting transfers between devices, swapped_far(): return lax.all_to_all(parts, FAR, 0, 0, tiled=True)  17.4 us
    all_to_all x1, blocking collectives, body(): lax.all_to_all(stats, STATS_FAR, 0, 0, tiled=True)  14.9 us
    ppermute x1, waiting for transfers between devices, body(): got = lax.ppermute(sent, HEAD, SWAP)  7.74 us
    all_to_all x1, waiting for transfers between devices, swapped_far(): return lax.all_to_all(parts, FAR, 0, 0, tiled=True)  7.62 us
    all_to_all x1, starting transfers between devices, body(): stats = lax.all_to_all(stats, STATS_NEAR, 0, 0, tiled=True)  5.91 us
    ppermute x1, starting transfers between devices, body(): late = lax.ppermute(kept_late, HEAD, SWAP)  4.54 us
  transfers between devices with their start and end apart: 6, of which 3 were waited for; matrix products, arithmetic and copies ran while one was open for 0% of the time, Pallas kernels for 8%

profile of v6, /device:TPU:1, one launch (start us, length us, event | category | flops | bytes accessed | tf_op | source)
XLA Modules:
  0.0 138.6 jit_solution(11490891007760265651)
XLA Ops:
  0.6 1.4 %broadcast_in_dim.4 = bf16[32,16,256]{2,1,0:T(8,128)(2,1)} broadcast(bf16[16,256]{1,0:T(8,128)(2,1)} %param.5), dimensions={1,2} | broadcast | bytes 270336 | tf_op jit(solution)/shard_map/broadcast_in_dim | solution.py:299
  2.1 17.4 %all-to-all-start = ((bf16[32,16,256]{2,1,0:T(8,128)(2,1)}), bf16[32,16,256]{2,1,0:T(8,128)(2,1)S(1)}, u32[]{:S(2)}, u32[]{:S(2)}) async-start(bf16[32,16,256]{2,1,0:T(8,128)(2,1)} %broadcast_in_dim.4), calls=%async_computation | async-start | bytes 524288 | tf_op jit(solution)/shard_map/all_to_all | solution.py:295
  19.5 0.1 pad_add_fusion.place
  19.6 0.0 copy-start
  19.6 2.4 %copy-done = bf16[4096,592]{0,1:T(8,128)(2,1)S(1)} copy-done((bf16[4096,592]{0,1:T(8,128)(2,1)S(1)}, bf16[4096,592]{0,1:T(8,128)(2,1)}, u32[]{:S(2)}) %copy-start) | copy-done | bytes 4849688
  22.0 2.9 %hold.1 = (bf16[592,2048]{1,0:T(8,128)(2,1)}, bf16[592,2048]{1,0:T(8,128)(2,1)}) custom-call(s32[3]{0:T(128)S(1)} %pad_add_fusion.place, bf16[592,4096]{1,0:T(8,128)(2,1)S(1)} %bitcast.16), custom_call_target="tpu_custom_call" | custom-call | tf_op jit(solution)/shard_map/hold/pallas_call | solution.py:50
  24.9 7.6 %all-to-all-done = bf16[32,16,256]{2,1,0:T(8,128)(2,1)S(1)} async-done(((bf16[32,16,256]{2,1,0:T(8,128)(2,1)}), bf16[32,16,256]{2,1,0:T(8,128)(2,1)S(1)}, u32[]{:S(2)}, u32[]{:S(2)}) %all-to-all-start) | async-done | bytes 262176 | tf_op jit(solution)/shard_map/all_to_all | solution.py:295
  32.5 0.1 broadcast_in_dim.5
  32.6 13.6 %all_to_all.30 = bf16[128,16,256]{2,1,0:T(8,128)(2,1)S(1)} all-to-all(bf16[128,16,256]{2,1,0:T(8,128)(2,1)S(1)} %bitcast.24), channel_id=1, replica_groups={{0,2,16,18},{4,6,20,22},{8,10,24,26},{12,14,28,30},{32,34,48,50},{36,38..., dimensions={0} | all-to-all | bytes 2097152 | tf_op jit(solution)/shard_map/all_to_all | solution.py:289
  46.2 3.1 %collective-permute-start = (bf16[128,16,256]{2,1,0:T(8,128)(2,1)S(1)}, bf16[128,16,256]{2,1,0:T(8,128)(2,1)S(1)}, u32[]{:S(2)}, u32[]{:S(2)}) collective-permute-start(bf16[128,16,256]{2,1,0:T(8,128)(2,1)S(1)} %all_to_all.30), channel_id=1, source_target_pairs={{0,1},{1,0},{2,3},{3,2},{4,5},{5,4},{6,7},{7,6},{8,9},{9,8},{10,11... | collective-permute-start | bytes 3145736 | tf_op jit(solution)/shard_map/ppermute | solution.py:318
  49.3 2.5 %first.1 = (f32[592,256]{1,0:T(8,128)S(1)}, bf16[592,2048]{1,0:T(8,128)(2,1)S(1)}) custom-call(bf16[2,2,2,4,4,16,256]{6,5,4,3,2,1,0:T(8,128)(2,1)S(1)} %bitcast.17, bf16[592,2048]{1,0:T(8,128)(2,1)} %get-tuple-element.25.w_mine, bf16[592,2048]{1,0:T(8,128)(2,1)} %get-tuple-element.33.w_other.weights), custom_call_target="tpu_custom_call" | custom-call | tf_op jit(solution)/shard_map/first/pallas_call | solution.py:322
  51.8 0.0 collective-permute-done
  51.8 1.4 %second.1 = (f32[592,128]{1,0:T(8,128)S(1)}, f32[592,128]{1,0:T(8,128)S(1)}) custom-call(s32[3]{0:T(128)S(1)} %pad_add_fusion.place, f32[592,256]{1,0:T(8,128)S(1)} %get-tuple-element.27.part, bf16[2,2,2,4,4,16,256]{6,5,4,3,2,1,0:T(8,128)(2,1)S(1)} %bitcast.19, bf16[592,2048]{1,0:T(8,128)(2,1)S(1)} %get-tuple-element.28.weights), custom_call_target="tpu_custom_call" | custom-call | tf_op jit(solution)/shard_map/second/pallas_call | solution.py:331
  53.2 4.4 %collective-permute-start.1 = (f32[592,128]{1,0:T(8,128)S(1)}, f32[592,128]{1,0:T(8,128)S(1)}, u32[]{:S(2)}, u32[]{:S(2)}) collective-permute-start(f32[592,128]{1,0:T(8,128)S(1)} %get-tuple-element.30.sent), channel_id=1, source_target_pairs={{0,256},{256,0},{1,257},{257,1},{2,258},{258,2},{3,259},{259,3},{4... | collective-permute-start | bytes 909320 | tf_op jit(solution)/shard_map/ppermute | solution.py:335
  57.6 7.7 %collective-permute-done.1.got = f32[592,128]{1,0:T(8,128)S(1)} collective-permute-done((f32[592,128]{1,0:T(8,128)S(1)}, f32[592,128]{1,0:T(8,128)S(1)}, u32[]{:S(2)}, u32[]{:S(2)}) %collective-permute-start.1) | collective-permute-done | bytes 303136 | tf_op jit(solution)/shard_map/ppermute | solution.py:335
  65.4 1.4 %stats.1 = f32[16,8,128]{2,1,0:T(8,128)} custom-call(s32[3]{0:T(128)S(1)} %pad_add_fusion.place, f32[592,128]{1,0:T(8,128)S(1)} %get-tuple-element.31.kept, f32[592,128]{1,0:T(8,128)S(1)} %collective-permute-done.1.got), custom_call_target="tpu_custom_call" | custom-call | tf_op jit(solution)/shard_map/stats/pallas_call | solution.py:337
  66.8 5.9 %all-to-all-start.2 = ((f32[16,8,128]{2,1,0:T(8,128)}), f32[16,8,128]{2,1,0:T(8,128)S(1)}, u32[]{:S(2)}, u32[]{:S(2)}) async-start(f32[16,8,128]{2,1,0:T(8,128)} %stats.1), calls=%async_computation.2 | async-start | bytes 131072 | tf_op jit(solution)/shard_map/all_to_all | solution.py:343
  72.7 0.0 copy-start.1
  72.7 0.0 copy-start.2
  72.8 0.0 copy-start.3
  72.8 4.5 %collective-permute-start.2 = (f32[592,128]{1,0:T(8,128)S(1)}, f32[592,128]{1,0:T(8,128)}, u32[]{:S(2)}, u32[]{:S(2)}) collective-permute-start(f32[592,128]{1,0:T(8,128)S(1)} %get-tuple-element.31.kept), channel_id=1, source_target_pairs={{0,256},{256,0},{1,257},{257,1},{2,258},{258,2},{3,259},{259,3},{4... | collective-permute-start | bytes 909320 | tf_op jit(solution)/shard_map/ppermute | solution.py:339
  77.3 1.7 %fetch.1.w_other = bf16[592,2048]{1,0:T(8,128)(2,1)S(1)} custom-call(bf16[592,2048]{1,0:T(8,128)(2,1)} %get-tuple-element.33.w_other.weights), custom_call_target="tpu_custom_call" | custom-call | tf_op jit(solution)/shard_map/fetch/pallas_call | solution.py:340
  79.0 1.5 %all-to-all-done.2.tiles = f32[16,8,128]{2,1,0:T(8,128)S(1)} async-done(((f32[16,8,128]{2,1,0:T(8,128)}), f32[16,8,128]{2,1,0:T(8,128)S(1)}, u32[]{:S(2)}, u32[]{:S(2)}) %all-to-all-start.2) | async-done | bytes 65568 | tf_op jit(solution)/shard_map/all_to_all | solution.py:343
  80.6 14.9 %all_to_all.31 = f32[32,8,128]{2,1,0:T(8,128)S(1)} all-to-all(f32[32,8,128]{2,1,0:T(8,128)S(1)} %merge.1), channel_id=1, replica_groups=mesh['head'=2,'xlo'=2,'yhi'=4,'ylo'=2,'zhi'=4,'zlo'=2,'core'=2] {'head',..., dimensions={0} | all-to-all | bytes 262144 | tf_op jit(solution)/shard_map/all_to_all | solution.py:346
  95.5 0.6 final.1
  96.1 0.0 collective-permute-done.2.late
  96.1 0.0 copy-done.1
  96.1 0.0 copy-done.2
  96.1 0.0 copy-done.3
  96.1 2.5 %sent_part.1 = (bf16[256,640]{1,0:T(8,128)(2,1)S(1)}, bf16[256,2048]{1,0:T(8,128)(2,1)S(1)}) custom-call(s32[3]{0:T(128)S(1)} %pad_add_fusion.place, f32[592,128]{1,0:T(8,128)S(1)} %get-tuple-element.31.kept, f32[592,128]{1,0:T(8,128)S(1)} %collective-permute-done.1.got, f32[592,128]{1,0:T(8,128)S(1)} %get-tuple-element.30.sent, ...), custom_call_target="tpu_custom_call" | custom-call | tf_op jit(solution)/shard_map/sent_part/pallas_call | solution.py:354
  98.6 4.0 %collective-permute-start.3 = (bf16[256,2048]{1,0:T(8,128)(2,1)S(1)}, bf16[256,2048]{1,0:T(8,128)(2,1)S(1)}, u32[]{:S(2)}, u32[]{:S(2)}) collective-permute-start(bf16[256,2048]{1,0:T(8,128)(2,1)S(1)} %get-tuple-element.38), channel_id=1, source_target_pairs={{0,1},{1,0},{2,3},{3,2},{4,5},{5,4},{6,7},{7,6},{8,9},{9,8},{10,11... | collective-permute-start | bytes 3145736 | tf_op jit(solution)/shard_map/ppermute | solution.py:364
  102.6 2.7 %own.1.partial = f32[256,2048]{1,0:T(8,128)S(1)} custom-call(bf16[256,640]{1,0:T(8,128)(2,1)S(1)} %get-tuple-element.37.turned, bf16[592,2048]{1,0:T(8,128)(2,1)} %get-tuple-element.25.w_mine), custom_call_target="tpu_custom_call" | custom-call | tf_op jit(solution)/shard_map/own/pallas_call | solution.py:365
  105.3 0.0 collective-permute-done.3.back
  105.3 0.2 pair_sum.1
  105.5 13.6 %all_to_all.32 = bf16[128,16,256]{2,1,0:T(8,128)(2,1)S(1)} all-to-all(bf16[128,16,256]{2,1,0:T(8,128)(2,1)S(1)} %bitcast.18), channel_id=1, replica_groups={{0,2,16,18},{4,6,20,22},{8,10,24,26},{12,14,28,30},{32,34,48,50},{36,38..., dimensions={0} | all-to-all | bytes 2097152 | tf_op jit(solution)/shard_map/all_to_all | solution.py:289
  119.2 0.2 reduce_sum.21
  119.4 18.5 %all_to_all.33 = bf16[32,16,256]{2,1,0:T(8,128)(2,1)S(1)} all-to-all(bf16[32,16,256]{2,1,0:T(8,128)(2,1)S(1)} %reduce_sum.21), channel_id=1, replica_groups=mesh['head'=2,'xlo'=2,'yhi'=4,'ylo'=2,'zhi'=4,'zlo'=2,'core'=2] {'xlo','..., dimensions={0} | all-to-all | bytes 524288 | tf_op jit(solution)/shard_map/all_to_all | solution.py:295
  137.9 0.7 convert_reduce_fusion
  (1 shorter events, 0.0 us)
Async XLA Ops:
  2.1 30.4 %all-to-all-start = ((bf16[32,16,256]{2,1,0:T(8,128)(2,1)}), bf16[32,16,256]{2,1,0:T(8,128)(2,1)S(1)}, u32[]{:S(2)}, u32[]{:S(2)}) async-start(bf16[32,16,256]{2,1,0:T(8,128)(2,1)} %broadcast_in_dim.4), calls=%async_computation | async-start | bytes 524288 | tf_op jit(solution)/shard_map/all_to_all | solution.py:295
  19.6 2.4 %copy-start = (bf16[4096,592]{0,1:T(8,128)(2,1)S(1)}, bf16[4096,592]{0,1:T(8,128)(2,1)}, u32[]{:S(2)}) copy-start(bf16[4096,592]{0,1:T(8,128)(2,1)} %param.6) | copy-start | bytes 14548996
  46.2 5.6 %collective-permute-start = (bf16[128,16,256]{2,1,0:T(8,128)(2,1)S(1)}, bf16[128,16,256]{2,1,0:T(8,128)(2,1)S(1)}, u32[]{:S(2)}, u32[]{:S(2)}) collective-permute-start(bf16[128,16,256]{2,1,0:T(8,128)(2,1)S(1)} %all_to_all.30), channel_id=1, source_target_pairs={{0,1},{1,0},{2,3},{3,2},{4,5},{5,4},{6,7},{7,6},{8,9},{9,8},{10,11... | collective-permute-start | bytes 3145736 | tf_op jit(solution)/shard_map/ppermute | solution.py:318
  53.2 12.1 %collective-permute-start.1 = (f32[592,128]{1,0:T(8,128)S(1)}, f32[592,128]{1,0:T(8,128)S(1)}, u32[]{:S(2)}, u32[]{:S(2)}) collective-permute-start(f32[592,128]{1,0:T(8,128)S(1)} %get-tuple-element.30.sent), channel_id=1, source_target_pairs={{0,256},{256,0},{1,257},{257,1},{2,258},{258,2},{3,259},{259,3},{4... | collective-permute-start | bytes 909320 | tf_op jit(solution)/shard_map/ppermute | solution.py:335
  66.8 13.7 %all-to-all-start.2 = ((f32[16,8,128]{2,1,0:T(8,128)}), f32[16,8,128]{2,1,0:T(8,128)S(1)}, u32[]{:S(2)}, u32[]{:S(2)}) async-start(f32[16,8,128]{2,1,0:T(8,128)} %stats.1), calls=%async_computation.2 | async-start | bytes 131072 | tf_op jit(solution)/shard_map/all_to_all | solution.py:343
  72.7 23.4 %copy-start.1 = (s32[256]{0:T(256)S(1)}, s32[256]{0:T(256)}, u32[]{:S(2)}) copy-start(s32[256]{0:T(256)} %param.7) | copy-start | bytes 3076
  72.7 23.4 %copy-start.2 = (f32[256]{0:T(256)S(1)}, f32[256]{0:T(256)}, u32[]{:S(2)}) copy-start(f32[256]{0:T(256)} %param.8) | copy-start | bytes 3076
  72.8 23.3 %copy-start.3 = (f32[256]{0:T(256)S(1)}, f32[256]{0:T(256)}, u32[]{:S(2)}) copy-start(f32[256]{0:T(256)} %param.9) | copy-start | bytes 3076
  72.8 23.3 %collective-permute-start.2 = (f32[592,128]{1,0:T(8,128)S(1)}, f32[592,128]{1,0:T(8,128)}, u32[]{:S(2)}, u32[]{:S(2)}) collective-permute-start(f32[592,128]{1,0:T(8,128)S(1)} %get-tuple-element.31.kept), channel_id=1, source_target_pairs={{0,256},{256,0},{1,257},{257,1},{2,258},{258,2},{3,259},{259,3},{4... | collective-permute-start | bytes 909320 | tf_op jit(solution)/shard_map/ppermute | solution.py:339
  98.6 6.7 %collective-permute-start.3 = (bf16[256,2048]{1,0:T(8,128)(2,1)S(1)}, bf16[256,2048]{1,0:T(8,128)(2,1)S(1)}, u32[]{:S(2)}, u32[]{:S(2)}) collective-permute-start(bf16[256,2048]{1,0:T(8,128)(2,1)S(1)} %get-tuple-element.38), channel_id=1, source_target_pairs={{0,1},{1,0},{2,3},{3,2},{4,5},{5,4},{6,7},{7,6},{8,9},{9,8},{10,11... | collective-permute-start | bytes 3145736 | tf_op jit(solution)/shard_map/ppermute | solution.py:364
